TPU v7x, 32 devices: a whole 2x2x4 slice. The times are simulated.
32 devices in a mesh: lon: 8 (over z, y), lat: 4 (over x, core).
Axes of the slice: x: 2, y: 2, z: 4, core: 2. Of those that a mesh axis runs over, the one named last changes fastest.
Arguments:
- heat_anomaly: float32 [75, 32, 1024], P(None, 'lat', 'lon'), may hold values from -6 to 6
- saltiness_anomaly: float32 [75, 32, 1024], P(None, 'lat', 'lon'), may hold values from -6 to 6
- zonal_edge_current: float32 [75, 32, 1024], P(None, 'lat', 'lon'), may hold values from -3 to 3
- meridional_edge_current: float32 [75, 32, 1024], P(None, 'lat', 'lon'), may hold values from -3 to 3
- interface_mixing_coefficient: float32 [74, 32, 1024], P(None, 'lat', 'lon'), may hold values from 0.05 to 5
- ocean_layer_number: int32 [32, 1024], P('lat', 'lon'), may hold values from 0 to 75, as said below
Outputs:
- heat_next: float32 [75, 32, 1024], P(None, 'lat', 'lon')
- saltiness_next: float32 [75, 32, 1024], P(None, 'lat', 'lon')
- zonal_current_next: float32 [75, 32, 1024], P(None, 'lat', 'lon')
- meridional_current_next: float32 [75, 32, 1024], P(None, 'lat', 'lon')
Inputs may be any that keep to these rules, and one draw needn't show every extreme that they name: `ocean_layer_number`: 0 marks a land column.
All inputs are finite; a program needn't handle non-finite values.
Results may differ from a plain program's by a relative error of at most 0.0003.
Values sent between devices are 32-bit elements; how exact they have to be, the bound alone decides.
A program may use at most 64 MiB of HBM per device.

v0:
```python
import jax
import jax.numpy as jnp
from jax import lax
from jax.sharding import PartitionSpec as P

time_step = 0.2
diffusion = 0.5
viscosity = 0.5
vertical_viscosity = 0.5
pressure_coef = 0.05
coriolis_coef = 1.5
thermal_coef = 1.0
thermal_curve = 0.2
haline_coef = 0.8
cabbeling_coef = 0.1


def from_partner(block, axis, stride):
    count = lax.axis_size(axis)
    route = []
    for low in range(count):
        high = low | 1 << stride
        if high != low and high < count:
            route += [(low, high), (high, low)]
    return lax.ppermute(block, axis, route)


def padded(block, sides, width, periodic):
    for axis, dim in sides:
        count = lax.axis_size(axis)
        forward = [(i, i + 1) for i in range(count - 1)]
        if periodic:
            forward.append((count - 1, 0))
        backward = [(target, source) for source, target in forward]
        low = lax.ppermute(
            lax.slice_in_dim(block, block.shape[dim] - width, None, axis=dim), axis, forward
        )
        high = lax.ppermute(lax.slice_in_dim(block, 0, width, axis=dim), axis, backward)
        block = jnp.concatenate([low, block, high], axis=dim)
    return block


def tendencies(heat_grid_values, salt_field, eastward, northward, depth_field, coriolis):
    layer_number = heat_grid_values.shape[0]
    heights = jnp.arange(layer_number, dtype=jnp.float32)[:, None, None] + 0.5
    ocean = (heights < depth_field[None]).astype(jnp.float32)
    density = ocean * (
        -thermal_coef * (1.0 + 0.5 * thermal_curve * heat_grid_values) * heat_grid_values
        + haline_coef * salt_field
        - cabbeling_coef * heat_grid_values * salt_field
    )
    pressure = pressure_coef * (jnp.cumsum(density, axis=0) - 0.5 * density)
    east_open = ocean[:, 1:-1, :-1] * ocean[:, 1:-1, 1:]
    north_open = ocean[:, :-1, 1:-1] * ocean[:, 1:, 1:-1]
    ocean_mid = ocean[:, 1:-1, 1:-1]
    stars = []
    for tracer in (heat_grid_values, salt_field):
        flux_east = east_open * (
            eastward[:, 1:-1, :-1] * 0.5 * (tracer[:, 1:-1, :-1] + tracer[:, 1:-1, 1:])
            - diffusion * (tracer[:, 1:-1, 1:] - tracer[:, 1:-1, :-1])
        )
        flux_north = north_open * (
            northward[:, :-1, 1:-1] * 0.5 * (tracer[:, :-1, 1:-1] + tracer[:, 1:, 1:-1])
            - diffusion * (tracer[:, 1:, 1:-1] - tracer[:, :-1, 1:-1])
        )
        change = (
            flux_east[:, :, 1:]
            - flux_east[:, :, :-1]
            + flux_north[:, 1:, :]
            - flux_north[:, :-1, :]
        )
        stars.append(ocean_mid * (tracer[:, 1:-1, 1:-1] - time_step * change))
    east_mid = east_open[:, :, 1:]
    north_mid = north_open[:, 1:, :]
    zonal_mid = eastward[:, 1:-1, 1:-1]
    merid_mid = northward[:, 1:-1, 1:-1]
    north_avg = 0.25 * (
        merid_mid + northward[:, 1:-1, 2:] + northward[:, :-2, 1:-1] + northward[:, :-2, 2:]
    )
    east_avg = 0.25 * (
        zonal_mid + eastward[:, 1:-1, :-2] + eastward[:, 2:, 1:-1] + eastward[:, 2:, :-2]
    )
    zonal_laplacian = (
        eastward[:, 1:-1, 2:]
        + eastward[:, 1:-1, :-2]
        + eastward[:, 2:, 1:-1]
        + eastward[:, :-2, 1:-1]
        - 4.0 * zonal_mid
    )
    merid_laplacian = (
        northward[:, 1:-1, 2:]
        + northward[:, 1:-1, :-2]
        + northward[:, 2:, 1:-1]
        + northward[:, :-2, 1:-1]
        - 4.0 * merid_mid
    )
    press_mid = pressure[:, 1:-1, 1:-1]
    east_star = east_mid * (
        zonal_mid
        + time_step
        * (coriolis * north_avg - (pressure[:, 1:-1, 2:] - press_mid) + viscosity * zonal_laplacian)
    )
    north_star = north_mid * (
        merid_mid
        + time_step
        * (-coriolis * east_avg - (pressure[:, 2:, 1:-1] - press_mid) + viscosity * merid_laplacian)
    )
    return (stars[0], stars[1], east_star, north_star, ocean_mid, east_mid, north_mid)


def banded_thomas_elimination(coupling, source):
    layer_number = source.shape[0]
    upper_prime = []
    source_prime = []
    for level_index in range(layer_number):
        divisor = jnp.ones_like(source[level_index])
        numerator = source[level_index]
        if level_index > 0:
            lower_here = -time_step * coupling[level_index - 1]
            divisor = divisor - lower_here - lower_here * upper_prime[level_index - 1]
            numerator = numerator - lower_here * source_prime[level_index - 1]
        if level_index < layer_number - 1:
            upper_here = -time_step * coupling[level_index]
            divisor = divisor - upper_here
            upper_prime.append(upper_here / divisor)
        else:
            upper_prime.append(jnp.zeros_like(numerator))
        source_prime.append(numerator / divisor)
    solved = [None] * layer_number
    solved[layer_number - 1] = source_prime[layer_number - 1]
    for level_index in range(layer_number - 2, -1, -1):
        solved[level_index] = (
            source_prime[level_index] - upper_prime[level_index] * solved[level_index + 1]
        )
    return jnp.stack(solved, axis=0)


def fold_row(top_row):
    flipped = top_row[:, ::-1]
    exchanged = flipped
    for bit_index in range(lax.axis_size("lon").bit_length() - 1):
        exchanged = from_partner(exchanged, "lon", bit_index)
    return exchanged


def local(
    heat_anomaly,
    saltiness_anomaly,
    zonal_edge_current,
    meridional_edge_current,
    interface_mixing_coefficient,
    ocean_layer_number,
):
    layer_number = heat_anomaly.shape[0]
    parallel_number = heat_anomaly.shape[1]
    lat_count = lax.axis_size("lat")
    lat_place = lax.axis_index("lat")
    at_top = lat_place == lat_count - 1
    upright_sweeps = ocean_layer_number.astype(jnp.float32)[None]
    stacked_tracers = jnp.concatenate(
        [
            heat_anomaly,
            saltiness_anomaly,
            zonal_edge_current,
            meridional_edge_current,
            upright_sweeps,
        ],
        axis=0,
    )
    field_count = stacked_tracers.shape[0]
    parity = jnp.concatenate(
        [
            jnp.ones((2 * layer_number,), jnp.float32),
            -jnp.ones((2 * layer_number,), jnp.float32),
            jnp.ones((1,), jnp.float32),
        ]
    )[:, None]
    lat_extended = padded(stacked_tracers, (("lat", 1),), 1, False)
    mirror = fold_row(stacked_tracers[:, parallel_number - 1, :]) * parity
    ghost_row = jnp.where(at_top, mirror, lat_extended[:, parallel_number + 1, :])
    lat_extended = lat_extended.at[:, parallel_number + 1, :].set(ghost_row)
    extended = padded(lat_extended, (("lon", 2),), 1, True)
    ghost_row = extended[:, parallel_number + 1, :]
    shifted = jnp.concatenate([ghost_row[:, 1:], ghost_row[:, -1:]], axis=1)
    field_ids = jnp.arange(field_count)[:, None]
    is_zonal = (field_ids >= 2 * layer_number) & (field_ids < 3 * layer_number)
    fixed_row = jnp.where(jnp.logical_and(at_top, is_zonal), shifted, ghost_row)
    extended = extended.at[:, parallel_number + 1, :].set(fixed_row)
    heat_grid_values = extended[:layer_number]
    salt_field = extended[layer_number : 2 * layer_number]
    eastward = extended[2 * layer_number : 3 * layer_number]
    northward = extended[3 * layer_number : 4 * layer_number]
    depth_field = extended[4 * layer_number]
    row_centres = (lat_place * parallel_number + jnp.arange(parallel_number)).astype(jnp.float32)
    total_rows = parallel_number * lat_count
    coriolis = (coriolis_coef * (2.0 * (row_centres + 0.5) / total_rows - 1.0))[None, :, None]
    heat_interim_guess, salt_star, east_star, north_star, ocean_mid, east_mid, north_mid = (
        tendencies(heat_grid_values, salt_field, eastward, northward, depth_field, coriolis)
    )
    scalar_coupling_coefs = interface_mixing_coefficient * ocean_mid[1:]
    coupling = jnp.stack(
        [
            scalar_coupling_coefs,
            scalar_coupling_coefs,
            vertical_viscosity * east_mid[1:],
            vertical_viscosity * north_mid[1:],
        ],
        axis=1,
    )
    sources = jnp.stack([heat_interim_guess, salt_star, east_star, north_star], axis=1)
    solved = banded_thomas_elimination(coupling, sources)
    return (solved[:, 0], solved[:, 1], solved[:, 2], solved[:, 3])


def solution(mesh):
    placed = (
        P(None, "lat", "lon"),
        P(None, "lat", "lon"),
        P(None, "lat", "lon"),
        P(None, "lat", "lon"),
        P(None, "lat", "lon"),
        P("lat", "lon"),
    )
    return jax.shard_map(
        local,
        mesh=mesh,
        in_specs=placed,
        out_specs=(
            P(None, "lat", "lon"),
            P(None, "lat", "lon"),
            P(None, "lat", "lon"),
            P(None, "lat", "lon"),
        ),
        check_vma=False,
    )
```

profile of v0, /device:TPU:0, one launch (start us, length us, event | category | flops | bytes accessed | tf_op | source)
XLA Modules:
  0.0 77.7 jit_solution(9172493850742309687)
XLA Ops:
  0.7 1.2 %copy.916 = f32[75,8,128]{0,2,1:T(8,128)S(1)} copy(f32[75,8,128]{2,1,0:T(8,128)} %param.10) | data formatting | bytes 614400 | tf_op args[0]
  1.9 1.2 %copy.917 = f32[75,8,128]{0,2,1:T(8,128)S(1)} copy(f32[75,8,128]{2,1,0:T(8,128)} %param.11) | data formatting | bytes 614400 | tf_op args[1]
  3.1 0.2 copy.918
  3.4 1.1 %copy.919 = f32[75,8,128]{0,2,1:T(8,128)} copy(f32[75,8,128]{2,1,0:T(8,128)S(1)} %copy-done.2) | data formatting | bytes 614400 | tf_op args[3]
  4.4 1.0 %copy.920 = f32[1,8,128]{0,2,1:T(8,128)} copy(f32[1,8,128]{2,1,0:T(8,128)S(1)} %convert_bitcast_fusion) | data formatting | bytes 8192 | tf_op jit(solution)/shard_map/broadcast_in_dim | solution.py:159
  5.5 2.0 %concatenate.21 = f32[301,8,128]{0,2,1:T(8,128)S(1)} concatenate(f32[75,8,128]{0,2,1:T(8,128)S(1)} %copy.916, f32[75,8,128]{0,2,1:T(8,128)S(1)} %copy.917, f32[75,8,128]{0,2,1:T(8,128)S(1)} %copy.918, f32[75,8,128]{0,2,1:T(8,128)} %copy.919, f32[1,8,128]{0,2,1:T(8,128)} %copy.920), dimensions={0} | concatenate | bytes 2465792 | tf_op jit(solution)/shard_map/concatenate | solution.py:160
  7.6 0.1 rev.3
  7.7 3.0 %collective-permute-start.2 = (f32[301,128]{0,1:T(8,128)S(1)}, f32[301,128]{0,1:T(8,128)S(1)}, u32[]{:S(2)}, u32[]{:S(2)}) collective-permute-start(f32[301,128]{0,1:T(8,128)S(1)} %rev.3), channel_id=1, source_target_pairs={{0,4},{4,0},{8,12},{12,8},{16,20},{20,16},{24,28},{28,24},{1,5},{5... | collective-permute-start | bytes 462344 | tf_op jit(solution)/shard_map/ppermute | solution.py:25
  10.7 1.3 %collective-permute-start.1 = (f32[301,1,128]{0,2,1:T(8,128)S(1)}, f32[301,1,128]{0,2,1:T(8,128)S(1)}, u32[]{:S(2)}, u32[]{:S(2)}) collective-permute-start(f32[301,1,128]{0,2,1:T(8,128)S(1)} %get-tuple-element.263), channel_id=1, source_target_pairs={{1,0},{2,1},{3,2},{5,4},{6,5},{7,6},{9,8},{10,9},{11,10},{13,12},{... | collective-permute-start | bytes 462344 | tf_op jit(solution)/shard_map/ppermute | solution.py:38
  12.0 3.0 %collective-permute-start = (f32[301,1,128]{0,2,1:T(8,128)S(1)}, f32[301,1,128]{0,2,1:T(8,128)S(1)}, u32[]{:S(2)}, u32[]{:S(2)}) collective-permute-start(f32[301,1,128]{0,2,1:T(8,128)S(1)} %get-tuple-element.264), channel_id=1, source_target_pairs={{0,1},{1,2},{2,3},{4,5},{5,6},{6,7},{8,9},{9,10},{10,11},{12,13},{... | collective-permute-start | bytes 462344 | tf_op jit(solution)/shard_map/ppermute | solution.py:35
  15.0 0.6 collective-permute-done.2
  15.6 1.8 %collective-permute-start.3 = (f32[301,128]{0,1:T(8,128)S(1)}, f32[301,128]{0,1:T(8,128)S(1)}, u32[]{:S(2)}, u32[]{:S(2)}) collective-permute-start(f32[301,128]{0,1:T(8,128)S(1)} %collective-permute-done.2), channel_id=1, source_target_pairs={{0,8},{8,0},{4,12},{12,4},{16,24},{24,16},{20,28},{28,20},{1,9},{9... | collective-permute-start | bytes 462344 | tf_op jit(solution)/shard_map/ppermute | solution.py:25
  17.4 5.6 %collective-permute-done.3 = f32[301,128]{0,1:T(8,128)S(1)} collective-permute-done((f32[301,128]{0,1:T(8,128)S(1)}, f32[301,128]{0,1:T(8,128)S(1)}, u32[]{:S(2)}, u32[]{:S(2)}) %collective-permute-start.3) | collective-permute-done | bytes 154144 | tf_op jit(solution)/shard_map/ppermute | solution.py:25
  23.0 2.6 %collective-permute-start.4 = (f32[301,128]{0,1:T(8,128)S(1)}, f32[301,128]{0,1:T(8,128)S(1)}, u32[]{:S(2)}, u32[]{:S(2)}) collective-permute-start(f32[301,128]{0,1:T(8,128)S(1)} %collective-permute-done.3), channel_id=1, source_target_pairs={{0,16},{16,0},{4,20},{20,4},{8,24},{24,8},{12,28},{28,12},{1,17},{... | collective-permute-start | bytes 462344 | tf_op jit(solution)/shard_map/ppermute | solution.py:25
  25.7 0.1 pad_maximum_fusion.1
  25.8 9.0 %collective-permute-done.4 = f32[301,128]{0,1:T(8,128)S(1)} collective-permute-done((f32[301,128]{0,1:T(8,128)S(1)}, f32[301,128]{0,1:T(8,128)S(1)}, u32[]{:S(2)}, u32[]{:S(2)}) %collective-permute-start.4) | collective-permute-done | bytes 154144 | tf_op jit(solution)/shard_map/ppermute | solution.py:25
  34.9 2.1 %collective-permute-start.6 = (f32[301,10,1]{0,2,1:T(1,128)S(1)}, f32[301,10,1]{0,2,1:T(1,128)S(1)}, u32[]{:S(2)}, u32[]{:S(2)}) collective-permute-start(f32[301,10,1]{0,2,1:T(1,128)S(1)} %get-tuple-element.261), channel_id=1, source_target_pairs={{4,0},{8,4},{12,8},{16,12},{20,16},{24,20},{28,24},{0,28},{5,1},{9... | collective-permute-start | bytes 36128 | tf_op jit(solution)/shard_map/ppermute | solution.py:38
  37.0 1.7 %collective-permute-done.6 = f32[301,10,1]{0,2,1:T(1,128)S(1)} collective-permute-done((f32[301,10,1]{0,2,1:T(1,128)S(1)}, f32[301,10,1]{0,2,1:T(1,128)S(1)}, u32[]{:S(2)}, u32[]{:S(2)}) %collective-permute-start.6) | collective-permute-done | bytes 12072 | tf_op jit(solution)/shard_map/ppermute | solution.py:38
  38.6 4.7 %collective-permute-done.5 = f32[301,10,1]{0,2,1:T(1,128)S(1)} collective-permute-done((f32[301,10,1]{0,2,1:T(1,128)S(1)}, f32[301,10,1]{0,2,1:T(1,128)S(1)}, u32[]{:S(2)}, u32[]{:S(2)}) %collective-permute-start.5) | collective-permute-done | bytes 12072 | tf_op jit(solution)/shard_map/ppermute | solution.py:35
  43.4 0.2 pad_maximum_fusion
  43.6 5.5 %copy.925 = f32[301,10,130]{2,1,0:T(8,128)} copy(f32[301,10,130]{0,2,1:T(8,128)S(1)} %pad_maximum_fusion) | data formatting | bytes 3130400 | tf_op jit(solution)/shard_map/concatenate | solution.py:39
  49.1 2.0 %slice.994 = f32[301,1,130]{2,1,0:T(1,128)S(1)} slice(f32[301,10,130]{2,1,0:T(8,128)} %copy.925), slice={[0:301], [9:10], [0:130]} | slice | bytes 313040 | tf_op jit(solution)/shard_map/slice | solution.py:183
  51.1 0.1 copy.922
  51.2 0.1 copy.924
  51.4 0.2 copy.923
  51.6 2.8 %broadcast_select_fusion = f32[301,1,130]{2,1,0:T(1,128)S(1)} fusion(pred[301]{0:T(512)(128)(4,1)S(1)} %fusion.384, f32[301,1,1]{2,1,0:T(1,128)S(1)} %copy.924, f32[301,1,129]{2,1,0:T(1,128)S(1)} %copy.923, f32[301,10,130]{2,1,0:T(8,128)} %copy.925), kind=kLoop, calls=%fused_computation.7 | loop fusion | flops 78260 | bytes 469861 | tf_op jit(solution)/shard_map/jit(_where)/select_n | solution.py:187
  54.4 8.3 %scatter.9 = f32[301,10,130]{2,1,0:T(8,128)} dynamic-update-slice(f32[301,10,130]{2,1,0:T(8,128)} %copy.925, f32[301,1,130]{2,1,0:T(1,128)S(1)} %broadcast_select_fusion, s32[]{:T(128)} %constant.90.clone.1, s32[]{:T(128)} %constant.91.clone.1, s32[]{:T(128)} %constant.90.clone.1) | dynamic-update-slice | bytes 313044 | tf_op jit(solution)/shard_map/scatter | solution.py:188
  62.7 0.7 slice_bitcast_fusion.5
  63.4 3.9 %subtract_multiply_fusion = f32[75,10,130]{2,1,0:T(8,128)S(1)} fusion(f32[301,10,130]{2,1,0:T(8,128)} %scatter.9, f32[10,130]{1,0:T(8,128)S(1)} %slice_bitcast_fusion.5, f32[75]{0:T(128)S(1)} %iota_add_fusion), kind=kOutput, calls=%fused_computation.5 | output fusion | flops 9457500 | bytes 5338992 | tf_op jit(solution)/shard_map/jit(cumsum)/reduce_window_sum | solution.py:52
  67.3 0.1 compare_convert_fusion
  67.5 0.1 copy-done
  67.6 0.9 %subtract_multiply_fusion.3 = (f32[75,9,128]{2,1,0:T(8,128)S(1)}, f32[75,9,128]{2,1,0:T(8,128)S(1)}) fusion(f32[301,10,130]{2,1,0:T(8,128)S(1)} %copy-done, f32[75,10,130]{2,1,0:T(8,128)S(1)} %compare_convert_fusion), kind=kLoop, calls=%fused_computation.14 | loop fusion | flops 691200 | bytes 2419200 | tf_op jit(solution)/shard_map/mul | solution.py:62
  68.5 0.5 subtract_multiply_fusion.4
  69.0 0.5 subtract_multiply_fusion.1
  69.6 0.4 subtract_multiply_fusion.2
  69.9 0.1 fusion.28
  70.1 0.7 fusion.7
  70.8 0.9 %fusion.16 = f32[75,1,8,128]{3,2,0,1:T(8,128)S(1)} fusion(f32[301,10,130]{2,1,0:T(8,128)S(1)} %copy-done, f32[75,10,130]{2,1,0:T(8,128)S(1)} %subtract_multiply_fusion, f32[75,8,129]{2,1,0:T(8,128)S(1)} %get-tuple-element.255, f32[8]{0:T(128)S(1)} %get-tuple-element.270), kind=kLoop, calls=%fused_computation.41 | loop fusion | flops 1228800 | bytes 3993632 | tf_op jit(solution)/shard_map/stack | solution.py:210
  71.8 0.2 fusion.30
  72.0 0.8 bitcast_divide_fusion.2
  72.8 0.6 fusion.27
  73.3 0.1 pad_maximum_fusion.2
  73.5 0.5 fusion.128
  74.0 0.1 fusion.185
  74.1 0.5 fusion.63
  74.6 0.4 constant_dynamic-update-slice_fusion.74
  75.1 0.7 constant_dynamic-update-slice_fusion.62
  76.7 1.0 %slice_bitcast_fusion = (f32[75,8,128]{2,1,0:T(8,128)}, f32[75,8,128]{2,1,0:T(8,128)}, f32[75,8,128]{2,1,0:T(8,128)}, f32[75,8,128]{2,1,0:T(8,128)}) fusion(f32[75,4,8,128]{3,2,0,1:T(8,128)S(1)} %constant_dynamic-update-slice_fusion), kind=kLoop, calls=%fused_computation.16 | loop fusion | bytes 2457600 | tf_op jit(solution)/shard_map/squeeze | solution.py:212
  (97 shorter events, 0.7 us)
Async XLA Ops:
  0.6 2.5 %copy-start.1 = (f32[75,8,128]{2,1,0:T(8,128)S(1)}, f32[75,8,128]{2,1,0:T(8,128)}, u32[]{:S(2)}) copy-start(f32[75,8,128]{2,1,0:T(8,128)} %param.12) | copy-start | bytes 921604
  0.6 2.7 %copy-start.2 = (f32[75,8,128]{2,1,0:T(8,128)S(1)}, f32[75,8,128]{2,1,0:T(8,128)}, u32[]{:S(2)}) copy-start(f32[75,8,128]{2,1,0:T(8,128)} %param.13) | copy-start | bytes 921604
  1.9 2.5 %copy-start.4 = (s32[8,128]{1,0:T(8,128)S(1)}, s32[8,128]{1,0:T(8,128)}, u32[]{:S(2)}) copy-start(s32[8,128]{1,0:T(8,128)} %param.15) | copy-start | bytes 12292
  7.7 7.9 %collective-permute-start.2 = (f32[301,128]{0,1:T(8,128)S(1)}, f32[301,128]{0,1:T(8,128)S(1)}, u32[]{:S(2)}, u32[]{:S(2)}) collective-permute-start(f32[301,128]{0,1:T(8,128)S(1)} %rev.3), channel_id=1, source_target_pairs={{0,4},{4,0},{8,12},{12,8},{16,20},{20,16},{24,28},{28,24},{1,5},{5... | collective-permute-start | bytes 462344 | tf_op jit(solution)/shard_map/ppermute | solution.py:25
  10.7 15.0 %collective-permute-start.1 = (f32[301,1,128]{0,2,1:T(8,128)S(1)}, f32[301,1,128]{0,2,1:T(8,128)S(1)}, u32[]{:S(2)}, u32[]{:S(2)}) collective-permute-start(f32[301,1,128]{0,2,1:T(8,128)S(1)} %get-tuple-element.263), channel_id=1, source_target_pairs={{1,0},{2,1},{3,2},{5,4},{6,5},{7,6},{9,8},{10,9},{11,10},{13,12},{... | collective-permute-start | bytes 462344 | tf_op jit(solution)/shard_map/ppermute | solution.py:38
  12.0 13.7 %collective-permute-start = (f32[301,1,128]{0,2,1:T(8,128)S(1)}, f32[301,1,128]{0,2,1:T(8,128)S(1)}, u32[]{:S(2)}, u32[]{:S(2)}) collective-permute-start(f32[301,1,128]{0,2,1:T(8,128)S(1)} %get-tuple-element.264), channel_id=1, source_target_pairs={{0,1},{1,2},{2,3},{4,5},{5,6},{6,7},{8,9},{9,10},{10,11},{12,13},{... | collective-permute-start | bytes 462344 | tf_op jit(solution)/shard_map/ppermute | solution.py:35
  15.6 7.4 %collective-permute-start.3 = (f32[301,128]{0,1:T(8,128)S(1)}, f32[301,128]{0,1:T(8,128)S(1)}, u32[]{:S(2)}, u32[]{:S(2)}) collective-permute-start(f32[301,128]{0,1:T(8,128)S(1)} %collective-permute-done.2), channel_id=1, source_target_pairs={{0,8},{8,0},{4,12},{12,4},{16,24},{24,16},{20,28},{28,20},{1,9},{9... | collective-permute-start | bytes 462344 | tf_op jit(solution)/shard_map/ppermute | solution.py:25
  17.4 17.4 %copy-start.5 = (f32[301]{0:T(512)S(1)}, f32[301]{0:T(512)}, u32[]{:S(2)}) copy-start(f32[301]{0:T(512)} %constant.89.clone.1) | copy-start | bytes 3616
  23.0 11.8 %collective-permute-start.4 = (f32[301,128]{0,1:T(8,128)S(1)}, f32[301,128]{0,1:T(8,128)S(1)}, u32[]{:S(2)}, u32[]{:S(2)}) collective-permute-start(f32[301,128]{0,1:T(8,128)S(1)} %collective-permute-done.3), channel_id=1, source_target_pairs={{0,16},{16,0},{4,20},{20,4},{8,24},{24,8},{12,28},{28,12},{1,17},{... | collective-permute-start | bytes 462344 | tf_op jit(solution)/shard_map/ppermute | solution.py:25
  34.9 3.8 %collective-permute-start.6 = (f32[301,10,1]{0,2,1:T(1,128)S(1)}, f32[301,10,1]{0,2,1:T(1,128)S(1)}, u32[]{:S(2)}, u32[]{:S(2)}) collective-permute-start(f32[301,10,1]{0,2,1:T(1,128)S(1)} %get-tuple-element.261), channel_id=1, source_target_pairs={{4,0},{8,4},{12,8},{16,12},{20,16},{24,20},{28,24},{0,28},{5,1},{9... | collective-permute-start | bytes 36128 | tf_op jit(solution)/shard_map/ppermute | solution.py:38
  37.0 6.4 %collective-permute-start.5 = (f32[301,10,1]{0,2,1:T(1,128)S(1)}, f32[301,10,1]{0,2,1:T(1,128)S(1)}, u32[]{:S(2)}, u32[]{:S(2)}) collective-permute-start(f32[301,10,1]{0,2,1:T(1,128)S(1)} %get-tuple-element.260), channel_id=1, source_target_pairs={{0,4},{4,8},{8,12},{12,16},{16,20},{20,24},{24,28},{28,0},{1,5},{5... | collective-permute-start | bytes 36128 | tf_op jit(solution)/shard_map/ppermute | solution.py:35
  63.4 4.2 %copy-start = (f32[301,10,130]{2,1,0:T(8,128)S(1)}, f32[301,10,130]{2,1,0:T(8,128)}, u32[]{:S(2)}) copy-start(f32[301,10,130]{2,1,0:T(8,128)} %scatter.9) | copy-start | bytes 4695604
  70.8 1.0 %copy-start.3 = (f32[74,8,128]{2,1,0:T(8,128)S(1)}, f32[74,8,128]{2,1,0:T(8,128)}, u32[]{:S(2)}) copy-start(f32[74,8,128]{2,1,0:T(8,128)} %param.14) | copy-start | bytes 909316
where the time goes:
time: 78.3 us; the launch traced here: 77.7 us
  local copies, waits for them, and re-layouts  25.2 us (32%)
  waiting for transfers between devices  21.6 us (28%)
  other arithmetic  15.6 us (20%)
  starting transfers between devices  13.9 us (18%)
  between operations  1.45 us (2%)
    ppermute x3, waiting for transfers between devices, from_partner(): return lax.ppermute(block, axis, route)  15.2 us
    scatter x1, local copies, waits for them, and re-layouts, local(): extended = extended.at[:, parallel_number + 1, :].set(fixed_row)  8.25 us
    ppermute x3, starting transfers between devices, from_partner(): return lax.ppermute(block, axis, route)  7.45 us
    concatenate x1, local copies, waits for them, and re-layouts, padded(): block = jnp.concatenate([low, block, high], axis=dim)  5.52 us
    ppermute x2, waiting for transfers between devices, padded(): lax.ppermute(lax.slice_in_dim(block, block.shape[dim] - width, None, axis...  4.74 us
    unnamed x53, local copies, waits for them, and re-layouts  3.99 us
    another operation x1, other arithmetic, tendencies(): pressure = pressure_coef * (jnp.cumsum(density, axis=0) - 0.5 * density)  3.95 us
    ppermute x2, starting transfers between devices, padded(): lax.ppermute(lax.slice_in_dim(block, 0, width, axis=dim), axis, backward)  3.37 us
  transfers between devices with their start and end apart: 7, of which 5 were waited for; matrix products, arithmetic and copies ran while one was open for 0% of the time, Pallas kernels for 0%

commit v1 on v0

v1 whole, which is shorter than its diff:
```python
import functools

import numpy as np
import jax
import jax.numpy as jnp
from jax import lax
from jax.experimental import pallas as pl
from jax.experimental.pallas import tpu as pltpu
from jax.sharding import PartitionSpec as P

MESH = pl.DeviceIdType.MESH
F32 = jnp.float32

time_step = 0.2
coriolis_coef = 1.5
pressure_coef = 0.05


def exchange_kernel(lon_n, lat_n, t_ref, s_ref, u_ref, v_ref, h_ref,
                    rows_ref, cols_ref, corner_ref,
                    row_send, col_send, row_ss, row_rs, col_ss, col_rs, cor_ss, cor_rs, fold_ss):
    levels, height, width = t_ref.shape
    fields = (t_ref, s_ref, u_ref, v_ref)
    lon = lax.axis_index("lon")
    lat = lax.axis_index("lat")
    east = lax.rem(lon + 1, lon_n)
    west = lax.rem(lon + lon_n - 1, lon_n)
    mirror = lon_n - 1 - lon
    second = lax.rem(2 * lon_n - 2 - lon, lon_n)
    top = lat == lat_n - 1
    has_south = lat > 0
    far = jnp.logical_and(top, second != lon)

    barrier = pltpu.get_barrier_semaphore()

    def greet(lon_to, lat_to):
        pl.semaphore_signal(barrier, inc=1, device_id={"lon": lon_to, "lat": lat_to}, device_id_type=MESH)

    greet(east, lat)
    greet(west, lat)

    @pl.when(has_south)
    def _():
        greet(lon, lat - 1)
        greet(east, lat - 1)

    @pl.when(jnp.logical_not(top))
    def _():
        greet(lon, lat + 1)
        greet(west, lat + 1)

    @pl.when(top)
    def _():
        greet(mirror, lat)

    @pl.when(far)
    def _():
        greet(second, lat)

    depth = h_ref[...].astype(F32)
    for f, ref in enumerate(fields):
        row_send[0, f, :levels, :] = ref[:, 0, :]
        row_send[1, f, :levels, :] = ref[:, height - 1, :]
    row_send[0, 0, levels : levels + 1, :] = depth[:1]
    row_send[1, 0, levels : levels + 1, :] = depth[height - 1 :]
    lane = lax.broadcasted_iota(jnp.int32, (height, width), 1)
    zero = jnp.zeros((height, width), F32)

    def pack(k, packs):
        here = lane == k
        out = []
        for f, ref in enumerate(fields):
            x = ref[k]
            out.append(jnp.where(here, pltpu.roll(x, k + 1, 1), packs[2 * f]))
            out.append(jnp.where(here, pltpu.roll(x, k, 1), packs[2 * f + 1]))
        return tuple(out)

    packs = lax.fori_loop(0, levels, pack, (zero,) * 8, unroll=5)
    for f in range(4):
        for side in range(2):
            tile = packs[2 * f + side]
            if f == 0:
                tile = jnp.where(lane == levels, pltpu.roll(depth, levels + 1 - side, 1), tile)
            col_send[side, f] = tile

    def remote(src, dst, send_sem, recv_sem, lon_to, lat_to):
        return pltpu.make_async_remote_copy(
            src_ref=src, dst_ref=dst, send_sem=send_sem, recv_sem=recv_sem,
            device_id={"lon": lon_to, "lat": lat_to}, device_id_type=MESH)

    to_north = remote(row_send.at[1], rows_ref.at[1], row_ss.at[1], row_rs.at[1], lon, lat + 1)
    to_mirror = remote(row_send.at[1], rows_ref.at[0], row_ss.at[1], row_rs.at[0], mirror, lat)
    to_south = remote(row_send.at[0], rows_ref.at[0], row_ss.at[0], row_rs.at[0], lon, lat - 1)
    to_east = remote(col_send.at[0], cols_ref.at[0], col_ss.at[0], col_rs.at[0], east, lat)
    to_west = remote(col_send.at[1], cols_ref.at[1], col_ss.at[1], col_rs.at[1], west, lat)
    to_south_east = remote(col_send.at[0, 2], corner_ref.at[0], cor_ss.at[0], cor_rs.at[0], east, lat - 1)
    to_north_west = remote(col_send.at[1, 3], corner_ref.at[1], cor_ss.at[1], cor_rs.at[1], west, lat + 1)
    to_second = remote(col_send.at[0, 2], corner_ref.at[0], fold_ss, cor_rs.at[0], second, lat)

    peers = (2 + 2 * has_south.astype(jnp.int32) + 2 * jnp.logical_not(top).astype(jnp.int32)
             + top.astype(jnp.int32) + far.astype(jnp.int32))
    pl.semaphore_wait(barrier, peers)

    @pl.when(top)
    def _():
        to_mirror.start()

    @pl.when(jnp.logical_not(top))
    def _():
        to_north.start()

    @pl.when(has_south)
    def _():
        to_south.start()

    @pl.when(far)
    def _():
        to_second.start()

    @pl.when(jnp.logical_and(top, second == lon))
    def _():
        corner_ref[0] = col_send[0, 2]

    @pl.when(jnp.logical_not(top))
    def _():
        to_north_west.start()

    @pl.when(has_south)
    def _():
        to_south_east.start()

    to_east.start()
    to_west.start()

    to_east.wait()
    to_west.wait()

    @pl.when(has_south)
    def _():
        to_south.wait_send()
        to_south_east.wait_send()
        to_north.wait_recv()
        to_north_west.wait_recv()

    @pl.when(jnp.logical_not(top))
    def _():
        to_north.wait_send()
        to_north_west.wait_send()
        to_south_east.wait_recv()

    @pl.when(top)
    def _():
        to_mirror.wait_send()

    @pl.when(far)
    def _():
        to_second.wait_send()
        to_second.wait_recv()

    to_south.wait_recv()


def face_tables(levels):
    part = time_step * 0.5
    ahead, last, factor = [], [], [0.0]
    for k in range(levels):
        above = part * (1.0 - factor[k]) if k else 0.0
        ahead.append(1.0 / (1.0 + part + above))
        last.append(1.0 / (1.0 + above))
        factor.append(part * ahead[k])
    return [np.asarray(x, np.float32) for x in (ahead, last, factor)]


def at_level(table, k):
    steady = table[-1]
    value = jnp.float32(float(steady))
    for i in range(len(table)):
        if table[i] != steady:
            value = jnp.where(k == i, jnp.float32(float(table[i])), value)
    return value


def column_kernel(lat_n, t_ref, s_ref, u_ref, v_ref, mix_ref, h_ref, rows_ref, cols_ref, corner_ref,
                  to_ref, so_ref, uo_ref, vo_ref, north_ref, south_ref, w_ref):
    levels, height, width = t_ref.shape
    padded = rows_ref.shape[2]
    lat = lax.axis_index("lat")
    top = lat == lat_n - 1
    has_south = lat > 0
    lane = lax.broadcasted_iota(jnp.int32, (height, width), 1)
    row = lax.broadcasted_iota(jnp.int32, (height, width), 0)
    first_lane, last_lane = lane == 0, lane == width - 1
    first_row, last_row = row == 0, row == height - 1
    wide_lane = lax.broadcasted_iota(jnp.int32, (padded, width), 1)

    def lanes(x, index):
        return jnp.take_along_axis(x, index, axis=1)

    plain = jnp.where(top, width - 1 - wide_lane, wide_lane)
    sign = jnp.where(top, -1.0, 1.0).astype(F32)
    corner = jnp.where(top, corner_ref[0, height - 1 :, :], corner_ref[0, :1, :])
    corner = jnp.transpose(jnp.broadcast_to(corner, (width, width)))[:padded]
    north_ref[0] = lanes(rows_ref[0, 0], plain)
    north_ref[1] = lanes(rows_ref[0, 1], plain)
    zonal = lanes(rows_ref[0, 2], plain)
    left = pltpu.roll(zonal, width - 1, 1)
    right = pltpu.roll(zonal, 1, 1)
    here = jnp.where(top, jnp.where(wide_lane == width - 1, corner, left), zonal)
    behind = jnp.where(top, zonal, jnp.where(wide_lane == 0, corner, right))
    north_ref[2] = sign * here
    north_ref[3] = sign * lanes(rows_ref[0, 3], plain)
    north_ref[4] = sign * (here + behind)

    corner = jnp.transpose(jnp.broadcast_to(corner_ref[1, height - 1 :, :], (width, width)))[:padded]
    merid = rows_ref[1, 3]
    for f in range(4):
        south_ref[f] = jnp.where(has_south, rows_ref[1, f], 0.0)
    ahead = jnp.where(wide_lane == width - 1, corner, pltpu.roll(merid, width - 1, 1))
    south_ref[4] = jnp.where(has_south, merid + ahead, 0.0)

    def to_east(x, f, k):
        return jnp.where(last_lane, pltpu.roll(cols_ref[1, f], width - 1 - k, 1), pltpu.roll(x, width - 1, 1))

    def to_west(x, f, k):
        return jnp.where(first_lane, pltpu.roll(cols_ref[0, f], lax.rem(width - k, width), 1), pltpu.roll(x, 1, 1))

    def to_north(x, f, k):
        return jnp.where(last_row, north_ref[f, pl.ds(k, 1), :], pltpu.roll(x, height - 1, 0))

    def to_south(x, f, k):
        return jnp.where(first_row, south_ref[f, pl.ds(k, 1), :], pltpu.roll(x, 1, 0))

    depth = h_ref[...].astype(F32)
    east_depth = jnp.minimum(depth, to_east(depth, 0, levels))
    west_depth = jnp.minimum(depth, to_west(depth, 0, levels))
    north_depth = jnp.minimum(depth, to_north(depth, 0, levels))
    south_depth = jnp.minimum(depth, to_south(depth, 0, levels))

    centre = (lat * height + row).astype(F32) + 0.5
    coriolis = coriolis_coef * (2.0 * centre / (height * lat_n) - 1.0)
    spin = (0.25 * time_step) * coriolis
    tables = face_tables(levels)
    push = time_step * pressure_coef
    part = time_step * 0.5

    def density(t, s):
        return 0.8 * s - t * (1.0 + 0.1 * (t + s))

    def down(k, carry):
        heat, salt, zonal, merid, a, w, east_sum, north_sum = carry
        level = k.astype(F32) + 0.5
        t, s, u, v = t_ref[k], s_ref[k], u_ref[k], v_ref[k]
        te, tw, tn, ts = to_east(t, 0, k), to_west(t, 0, k), to_north(t, 0, k), to_south(t, 0, k)
        se, sw, sn, ss = to_east(s, 1, k), to_west(s, 1, k), to_north(s, 1, k), to_south(s, 1, k)
        ue, uw, un, us = to_east(u, 2, k), to_west(u, 2, k), to_north(u, 2, k), to_south(u, 2, k)
        ve, vw, vn, vs = to_east(v, 3, k), to_west(v, 3, k), to_north(v, 3, k), to_south(v, 3, k)
        uu, vv = u + uw, v + ve
        ubar = uu + to_north(uu, 4, k)
        vbar = vv + to_south(vv, 4, k)
        open_c = level < depth
        open_e, open_w = level < east_depth, level < west_depth
        open_n, open_s = level < north_depth, level < south_depth

        def face(mask, speed):
            x = part * speed
            return jnp.where(mask, part - x, 0.0), jnp.where(mask, part + x, 0.0)

        e_far, e_own = face(open_e, u)
        w_own, w_far = face(open_w, uw)
        n_far, n_own = face(open_n, v)
        s_own, s_far = face(open_s, vs)
        own = 1.0 - e_own - w_own - n_own - s_own
        t_star = own * t + e_far * te + w_far * tw + n_far * tn + s_far * ts
        s_star = own * s + e_far * se + w_far * sw + n_far * sn + s_far * ss

        rho = density(t, s)
        east_step = density(te, se) - rho
        north_step = density(tn, sn) - rho
        half_e = push * 0.5 * east_step
        half_n = push * 0.5 * north_step
        east_push = east_sum + half_e
        north_push = north_sum + half_n
        u_star = (1.0 - 4.0 * part) * u + part * (ue + uw + un + us) + spin * vbar - east_push
        v_star = (1.0 - 4.0 * part) * v + part * (ve + vw + vn + vs) - spin * ubar - north_push

        below = jnp.minimum(k, levels - 2)
        a_next = jnp.where(level + 1.0 < depth, time_step * mix_ref[below], 0.0)
        d = (1.0 + a_next + a) - a * w
        r = pl.reciprocal(d, approx=True)
        r = r * (2.0 - d * r)
        w_next = a_next * r
        heat = jnp.where(open_c, (t_star + a * heat) * r, 0.0)
        salt = jnp.where(open_c, (s_star + a * salt) * r, 0.0)
        r_ahead, r_last = at_level(tables[0], k), at_level(tables[1], k)
        r_e = jnp.where(level + 1.0 < east_depth, r_ahead, r_last)
        r_n = jnp.where(level + 1.0 < north_depth, r_ahead, r_last)
        zonal = jnp.where(open_e, (u_star + part * zonal) * r_e, 0.0)
        merid = jnp.where(open_n, (v_star + part * merid) * r_n, 0.0)
        to_ref[k] = heat
        so_ref[k] = salt
        uo_ref[k] = zonal
        vo_ref[k] = merid
        w_ref[k] = w_next
        return heat, salt, zonal, merid, a_next, w_next, east_push + half_e, north_push + half_n

    zero = jnp.zeros((height, width), F32)
    out = lax.fori_loop(0, levels, down, (zero,) * 8, unroll=3)

    def up(i, carry):
        heat, salt, zonal, merid = carry
        k = levels - 2 - i
        w = w_ref[k]
        wc = at_level(tables[2][1:], k)
        heat = to_ref[k] + w * heat
        salt = so_ref[k] + w * salt
        zonal = uo_ref[k] + wc * zonal
        merid = vo_ref[k] + wc * merid
        to_ref[k] = heat
        so_ref[k] = salt
        uo_ref[k] = zonal
        vo_ref[k] = merid
        return heat, salt, zonal, merid

    lax.fori_loop(0, levels - 1, up, out[:4], unroll=2)


def local(lon_n, lat_n, t, s, u, v, mix, h):
    levels, height, width = t.shape
    padded = (levels + 1 + 7) // 8 * 8
    vmem = pl.BlockSpec(memory_space=pltpu.VMEM)
    shape = functools.partial(jax.ShapeDtypeStruct, dtype=F32)
    dma = pltpu.SemaphoreType.DMA
    rows, cols, corners = pl.pallas_call(
        functools.partial(exchange_kernel, lon_n, lat_n),
        out_shape=(shape((2, 4, padded, width)), shape((2, 4, height, width)), shape((2, height, width))),
        in_specs=[vmem] * 5,
        out_specs=(vmem,) * 3,
        scratch_shapes=[
            pltpu.VMEM((2, 4, padded, width), F32),
            pltpu.VMEM((2, 4, height, width), F32),
            dma((2,)), dma((2,)), dma((2,)), dma((2,)), dma((2,)), dma((2,)), dma,
        ],
        compiler_params=pltpu.CompilerParams(
            collective_id=0, has_side_effects=True, vmem_limit_bytes=16 << 20),
    )(t, s, u, v, h)
    field = shape((levels, height, width))
    return pl.pallas_call(
        functools.partial(column_kernel, lat_n),
        out_shape=(field,) * 4,
        in_specs=[vmem] * 9,
        out_specs=(vmem,) * 4,
        scratch_shapes=[
            pltpu.VMEM((5, padded, width), F32),
            pltpu.VMEM((5, padded, width), F32),
            pltpu.VMEM((levels, height, width), F32),
        ],
        compiler_params=pltpu.CompilerParams(vmem_limit_bytes=32 << 20),
    )(t, s, u, v, mix, h, rows, cols, corners)


def solution(mesh):
    field = P(None, "lat", "lon")
    return jax.shard_map(
        functools.partial(local, mesh.shape["lon"], mesh.shape["lat"]),
        mesh=mesh,
        in_specs=(field,) * 5 + (P("lat", "lon"),),
        out_specs=(field,) * 4,
        check_vma=False,
    )
```

time: 78.3 us -> 21.8 us (0.28)
  the two profiles are of different devices: /device:TPU:0 before, /device:TPU:1 now
where the time goes in v1:
time: 21.8 us; the launch traced here: 21.5 us
  Pallas kernels  15.3 us (70%)
  local copies, waits for them, and re-layouts  5.52 us (25%)
  between operations  0.7 us (3%)
    pallas_call x1, Pallas kernels, local(): pl.pallas_call(functools.partial(exchange_kernel, lon_n, lat_n), out_shap...  10.3 us
    unnamed x20, local copies, waits for them, and re-layouts  5.52 us
    pallas_call x1, Pallas kernels, local(): pl.pallas_call(functools.partial(column_kernel, lat_n), out_shape=(field,...  4.99 us

profile of v1, /device:TPU:1, one launch (start us, length us, event | category | flops | bytes accessed | tf_op | source)
XLA Modules:
  0.0 21.5 jit_solution(8436901955051086385)
XLA Ops:
  0.6 0.0 copy-start
  0.6 1.0 %copy-done = f32[75,8,128]{2,1,0:T(8,128)S(1)} copy-done((f32[75,8,128]{2,1,0:T(8,128)S(1)}, f32[75,8,128]{2,1,0:T(8,128)}, u32[]{:S(2)}) %copy-start) | copy-done | bytes 307224
  1.6 0.0 copy-start.2
  1.6 1.0 %copy-done.2 = f32[75,8,128]{2,1,0:T(8,128)S(1)} copy-done((f32[75,8,128]{2,1,0:T(8,128)S(1)}, f32[75,8,128]{2,1,0:T(8,128)}, u32[]{:S(2)}) %copy-start.2) | copy-done | bytes 307224
  2.6 0.0 copy-start.4
  2.6 1.0 %copy-done.4 = f32[75,8,128]{2,1,0:T(8,128)S(1)} copy-done((f32[75,8,128]{2,1,0:T(8,128)S(1)}, f32[75,8,128]{2,1,0:T(8,128)}, u32[]{:S(2)}) %copy-start.4) | copy-done | bytes 307224
  3.5 0.0 copy-start.6
  3.5 1.0 %copy-done.6 = f32[75,8,128]{2,1,0:T(8,128)S(1)} copy-done((f32[75,8,128]{2,1,0:T(8,128)S(1)}, f32[75,8,128]{2,1,0:T(8,128)}, u32[]{:S(2)}) %copy-start.6) | copy-done | bytes 307224
  4.5 0.0 copy-start.9
  4.5 0.7 %copy-done.9 = s32[8,128]{1,0:T(8,128)S(1)} copy-done((s32[8,128]{1,0:T(8,128)S(1)}, s32[8,128]{1,0:T(8,128)}, u32[]{:S(2)}) %copy-start.9) | copy-done | bytes 4120
  5.2 0.0 copy-start.1
  5.2 0.0 copy-start.3
  5.2 0.0 copy-start.5
  5.2 0.0 copy-start.7
  5.2 10.3 %shard_map.93 = (f32[2,4,80,128]{3,2,1,0:T(8,128)S(1)}, f32[2,4,8,128]{3,2,1,0:T(8,128)S(1)}, f32[2,8,128]{2,1,0:T(8,128)S(1)}) custom-call(f32[75,8,128]{2,1,0:T(8,128)S(1)} %copy-done, f32[75,8,128]{2,1,0:T(8,128)S(1)} %copy-done.2, f32[75,8,128]{2,1,0:T(8,128)S(1)} %copy-done.4, f32[75,8,128]{2,1,0:T(8,128)S(1)} %copy-done.6, s32[8,128]{1,0:T(8,128)S(1)} %copy-done.9), custom_call_target="tpu_custom_call" | custom-call | tf_op jit(solution)/shard_map/pallas_call | solution.py:333
  15.5 0.0 copy-done.1
  15.5 0.0 copy-done.3
  15.5 0.0 copy-done.5
  15.5 0.0 copy-done.7
  15.5 0.0 copy-start.8
  15.5 1.0 %copy-done.8 = f32[74,8,128]{2,1,0:T(8,128)S(1)} copy-done((f32[74,8,128]{2,1,0:T(8,128)S(1)}, f32[74,8,128]{2,1,0:T(8,128)}, u32[]{:S(2)}) %copy-start.8) | copy-done | bytes 303128
  16.5 5.0 %shard_map.94 = (f32[75,8,128]{2,1,0:T(8,128)}, f32[75,8,128]{2,1,0:T(8,128)}, f32[75,8,128]{2,1,0:T(8,128)}, f32[75,8,128]{2,1,0:T(8,128)}) custom-call(f32[75,8,128]{2,1,0:T(8,128)S(1)} %copy-done.1, f32[75,8,128]{2,1,0:T(8,128)S(1)} %copy-done.3, f32[75,8,128]{2,1,0:T(8,128)S(1)} %copy-done.5, f32[75,8,128]{2,1,0:T(8,128)S(1)} %copy-done.7, ...), custom_call_target="tpu_custom_call" | custom-call | tf_op jit(solution)/shard_map/pallas_call | solution.py:347
Async XLA Ops:
  0.6 1.0 %copy-start = (f32[75,8,128]{2,1,0:T(8,128)S(1)}, f32[75,8,128]{2,1,0:T(8,128)}, u32[]{:S(2)}) copy-start(f32[75,8,128]{2,1,0:T(8,128)} %t_ref.3) | copy-start | bytes 921604
  1.6 1.0 %copy-start.2 = (f32[75,8,128]{2,1,0:T(8,128)S(1)}, f32[75,8,128]{2,1,0:T(8,128)}, u32[]{:S(2)}) copy-start(f32[75,8,128]{2,1,0:T(8,128)} %s_ref.3) | copy-start | bytes 921604
  2.6 1.0 %copy-start.4 = (f32[75,8,128]{2,1,0:T(8,128)S(1)}, f32[75,8,128]{2,1,0:T(8,128)}, u32[]{:S(2)}) copy-start(f32[75,8,128]{2,1,0:T(8,128)} %u_ref.3) | copy-start | bytes 921604
  3.5 1.0 %copy-start.6 = (f32[75,8,128]{2,1,0:T(8,128)S(1)}, f32[75,8,128]{2,1,0:T(8,128)}, u32[]{:S(2)}) copy-start(f32[75,8,128]{2,1,0:T(8,128)} %v_ref.3) | copy-start | bytes 921604
  4.5 0.7 %copy-start.9 = (s32[8,128]{1,0:T(8,128)S(1)}, s32[8,128]{1,0:T(8,128)}, u32[]{:S(2)}) copy-start(s32[8,128]{1,0:T(8,128)} %h_ref.3) | copy-start | bytes 12292
  5.2 10.3 %copy-start.1 = (f32[75,8,128]{2,1,0:T(8,128)S(1)}, f32[75,8,128]{2,1,0:T(8,128)}, u32[]{:S(2)}) copy-start(f32[75,8,128]{2,1,0:T(8,128)} %t_ref.3) | copy-start | bytes 921604
  5.2 10.3 %copy-start.3 = (f32[75,8,128]{2,1,0:T(8,128)S(1)}, f32[75,8,128]{2,1,0:T(8,128)}, u32[]{:S(2)}) copy-start(f32[75,8,128]{2,1,0:T(8,128)} %s_ref.3) | copy-start | bytes 921604
  5.2 10.3 %copy-start.5 = (f32[75,8,128]{2,1,0:T(8,128)S(1)}, f32[75,8,128]{2,1,0:T(8,128)}, u32[]{:S(2)}) copy-start(f32[75,8,128]{2,1,0:T(8,128)} %u_ref.3) | copy-start | bytes 921604
  5.2 10.3 %copy-start.7 = (f32[75,8,128]{2,1,0:T(8,128)S(1)}, f32[75,8,128]{2,1,0:T(8,128)}, u32[]{:S(2)}) copy-start(f32[75,8,128]{2,1,0:T(8,128)} %v_ref.3) | copy-start | bytes 921604
  15.5 1.0 %copy-start.8 = (f32[74,8,128]{2,1,0:T(8,128)S(1)}, f32[74,8,128]{2,1,0:T(8,128)}, u32[]{:S(2)}) copy-start(f32[74,8,128]{2,1,0:T(8,128)} %mix_ref.1) | copy-start | bytes 909316

commit v2 on v1

v2 whole, which is shorter than its diff:
```python
import functools

import numpy as np
import jax
import jax.numpy as jnp
from jax import lax
from jax.experimental import pallas as pl
from jax.experimental.pallas import tpu as pltpu
from jax.sharding import PartitionSpec as P

MESH = pl.DeviceIdType.MESH
F32 = jnp.float32

time_step = 0.2
coriolis_coef = 1.5
pressure_coef = 0.05


def face_tables(levels):
    part = time_step * 0.5
    ahead, last, factor = [], [], [0.0]
    for k in range(levels):
        above = part * (1.0 - factor[k]) if k else 0.0
        ahead.append(1.0 / (1.0 + part + above))
        last.append(1.0 / (1.0 + above))
        factor.append(part * ahead[k])
    return [np.asarray(x, np.float32) for x in (ahead, last, factor)]


def at_level(table, k):
    steady = table[-1]
    value = jnp.float32(float(steady))
    for i in range(len(table)):
        if table[i] != steady:
            value = jnp.where(k == i, jnp.float32(float(table[i])), value)
    return value


def chunks(levels, padded):
    size = padded // 3 // 8 * 8
    starts = [i * size for i in range(3)]
    stops = starts[1:] + [padded]
    return [(a, b, min(b, levels)) for a, b in zip(starts, stops)]


def forward_kernel(lon_n, lat_n, t_hbm, s_hbm, u_hbm, v_hbm, mix_hbm, h_hbm,
                   to_ref, so_ref, uo_ref, vo_ref, w_ref,
                   fields, mix, deep, deep_send, deep_got, row_send, rows, col_send, cols, corners,
                   north_ref, south_ref,
                   in_sem, deep_ss, deep_rs, row_ss, row_rs, col_ss, col_rs, cor_ss, cor_rs, fold_ss):
    levels, height, width = t_hbm.shape
    padded = rows.shape[2]
    parts = chunks(levels, padded)
    lon = lax.axis_index("lon")
    lat = lax.axis_index("lat")
    east = lax.rem(lon + 1, lon_n)
    west = lax.rem(lon + lon_n - 1, lon_n)
    mirror = lon_n - 1 - lon
    second = lax.rem(2 * lon_n - 2 - lon, lon_n)
    top = lat == lat_n - 1
    inner = jnp.logical_not(top)
    has_south = lat > 0
    far = jnp.logical_and(top, second != lon)

    loads = [pltpu.make_async_copy(src, dst, in_sem.at[i]) for i, (src, dst) in enumerate([
        (h_hbm, deep), (t_hbm, fields.at[0]), (s_hbm, fields.at[1]),
        (u_hbm, fields.at[2]), (v_hbm, fields.at[3]), (mix_hbm, mix)])]
    for load in loads:
        load.start()

    barrier = pltpu.get_barrier_semaphore()

    def greet(lon_to, lat_to):
        pl.semaphore_signal(barrier, inc=1, device_id={"lon": lon_to, "lat": lat_to}, device_id_type=MESH)

    @pl.when(top)
    def _():
        greet(mirror, lat)

    @pl.when(far)
    def _():
        greet(second, lat)

    greet(east, lat)
    greet(west, lat)

    @pl.when(has_south)
    def _():
        greet(lon, lat - 1)
        greet(east, lat - 1)

    @pl.when(inner)
    def _():
        greet(lon, lat + 1)
        greet(west, lat + 1)

    def remote(src, dst, send_sem, recv_sem, lon_to, lat_to):
        return pltpu.make_async_remote_copy(
            src_ref=src, dst_ref=dst, send_sem=send_sem, recv_sem=recv_sem,
            device_id={"lon": lon_to, "lat": lat_to}, device_id_type=MESH)

    def row_copy(c, own, slot, lon_to, lat_to):
        a, b, _ = parts[c]
        return remote(row_send.at[own, :, a:b], rows.at[slot, :, a:b], row_ss.at[own, c], row_rs.at[slot, c], lon_to, lat_to)

    to_north = [row_copy(c, 1, 1, lon, lat + 1) for c in range(3)]
    to_mirror = [row_copy(c, 1, 0, mirror, lat) for c in range(3)]
    to_south = [row_copy(c, 0, 0, lon, lat - 1) for c in range(3)]
    to_north.append(remote(deep_send, deep_got.at[1], deep_ss.at[1], deep_rs.at[1], lon, lat + 1))
    to_mirror.append(remote(deep_send, deep_got.at[0], deep_ss.at[1], deep_rs.at[0], mirror, lat))
    to_south.append(remote(deep_send, deep_got.at[0], deep_ss.at[0], deep_rs.at[0], lon, lat - 1))
    to_east = remote(col_send.at[0], cols.at[0], col_ss.at[0], col_rs.at[0], east, lat)
    to_west = remote(col_send.at[1], cols.at[1], col_ss.at[1], col_rs.at[1], west, lat)
    to_south_east = remote(col_send.at[0, 2], corners.at[0], cor_ss.at[0], cor_rs.at[0], east, lat - 1)
    to_north_west = remote(col_send.at[1, 3], corners.at[1], cor_ss.at[1], cor_rs.at[1], west, lat + 1)
    to_second = remote(col_send.at[0, 2], corners.at[0], fold_ss, cor_rs.at[0], second, lat)

    def send_rows(pieces):
        @pl.when(top)
        def _():
            for c in pieces:
                to_mirror[c].start()

        @pl.when(inner)
        def _():
            for c in pieces:
                to_north[c].start()

        @pl.when(has_south)
        def _():
            for c in pieces:
                to_south[c].start()

    loads[0].wait()
    depth = deep[...].astype(F32)
    deep_send[...] = depth
    for f in range(4):
        loads[1 + f].wait()
        row_send[0, f, :levels, :] = fields[f, :, 0, :]
        row_send[1, f, :levels, :] = fields[f, :, height - 1, :]

    peers = (2 + 2 * has_south.astype(jnp.int32) + 2 * inner.astype(jnp.int32)
             + top.astype(jnp.int32) + far.astype(jnp.int32))
    pl.semaphore_wait(barrier, peers)
    send_rows([3, 0])

    lane = lax.broadcasted_iota(jnp.int32, (height, width), 1)
    row = lax.broadcasted_iota(jnp.int32, (height, width), 0)
    zero = jnp.zeros((height, width), F32)

    def pack(k, packs):
        here = lane == k
        out = []
        for f in range(4):
            x = fields[f, k]
            out.append(jnp.where(here, pltpu.roll(x, k + 1, 1), packs[2 * f]))
            out.append(jnp.where(here, pltpu.roll(x, k, 1), packs[2 * f + 1]))
        return tuple(out)

    packs = lax.fori_loop(0, levels, pack, (zero,) * 8, unroll=5)
    for f in range(4):
        for side in range(2):
            tile = packs[2 * f + side]
            if f == 0:
                tile = jnp.where(lane == levels, pltpu.roll(depth, levels + 1 - side, 1), tile)
            col_send[side, f] = tile

    to_east.start()
    to_west.start()

    @pl.when(far)
    def _():
        to_second.start()

    @pl.when(jnp.logical_and(top, second == lon))
    def _():
        corners[0] = col_send[0, 2]

    @pl.when(inner)
    def _():
        to_north_west.start()

    @pl.when(has_south)
    def _():
        to_south_east.start()

    send_rows([1, 2])

    first_lane, last_lane = lane == 0, lane == width - 1
    first_row, last_row = row == 0, row == height - 1

    def lanes(x, index):
        return jnp.take_along_axis(x, index, axis=1)

    def turned(x):
        wide = lax.broadcasted_iota(jnp.int32, x.shape, 1)
        return lanes(x, jnp.where(top, width - 1 - wide, wide))

    sign = jnp.where(top, -1.0, 1.0).astype(F32)
    loads[5].wait()
    to_east.wait()
    to_west.wait()

    @pl.when(inner)
    def _():
        to_south_east.wait_recv()
        to_north_west.wait_send()

    @pl.when(has_south)
    def _():
        to_north_west.wait_recv()
        to_south_east.wait_send()
        to_north[3].wait_recv()

    @pl.when(far)
    def _():
        to_second.wait()

    to_south[3].wait_recv()
    north_deep = turned(jnp.where(top, pltpu.roll(deep_got[0], 1, 0), deep_got[0]))[:1]
    south_deep = jnp.where(has_south, deep_got[1], 0.0)[height - 1 :]
    north_corner = jnp.where(top, corners[0, height - 1 :, :], corners[0, :1, :])
    north_corner = jnp.transpose(jnp.broadcast_to(north_corner, (width, width)))[:padded]
    south_corner = jnp.transpose(jnp.broadcast_to(corners[1, height - 1 :, :], (width, width)))[:padded]

    def take_rows(c):
        a, b, _ = parts[c]
        to_south[c].wait_recv()

        @pl.when(has_south)
        def _():
            to_north[c].wait_recv()

        wide_lane = lax.broadcasted_iota(jnp.int32, (b - a, width), 1)
        corner = north_corner[a:b]
        north_ref[0, a:b] = turned(rows[0, 0, a:b])
        north_ref[1, a:b] = turned(rows[0, 1, a:b])
        zonal = turned(rows[0, 2, a:b])
        left = pltpu.roll(zonal, width - 1, 1)
        right = pltpu.roll(zonal, 1, 1)
        here = jnp.where(top, jnp.where(wide_lane == width - 1, corner, left), zonal)
        behind = jnp.where(top, zonal, jnp.where(wide_lane == 0, corner, right))
        north_ref[2, a:b] = sign * here
        north_ref[3, a:b] = sign * turned(rows[0, 3, a:b])
        north_ref[4, a:b] = sign * (here + behind)
        merid = rows[1, 3, a:b]
        for f in range(4):
            south_ref[f, a:b] = jnp.where(has_south, rows[1, f, a:b], 0.0)
        ahead = jnp.where(wide_lane == width - 1, south_corner[a:b], pltpu.roll(merid, width - 1, 1))
        south_ref[4, a:b] = jnp.where(has_south, merid + ahead, 0.0)

    def to_east_of(x, f, k):
        return jnp.where(last_lane, pltpu.roll(cols[1, f], width - 1 - k, 1), pltpu.roll(x, width - 1, 1))

    def to_west_of(x, f, k):
        return jnp.where(first_lane, pltpu.roll(cols[0, f], lax.rem(width - k, width), 1), pltpu.roll(x, 1, 1))

    def to_north_of(x, f, k):
        return jnp.where(last_row, north_ref[f, pl.ds(k, 1), :], pltpu.roll(x, height - 1, 0))

    def to_south_of(x, f, k):
        return jnp.where(first_row, south_ref[f, pl.ds(k, 1), :], pltpu.roll(x, 1, 0))

    east_depth = jnp.minimum(depth, to_east_of(depth, 0, levels))
    west_depth = jnp.minimum(depth, to_west_of(depth, 0, levels))
    north_depth = jnp.minimum(depth, jnp.where(last_row, north_deep, pltpu.roll(depth, height - 1, 0)))
    south_depth = jnp.minimum(depth, jnp.where(first_row, south_deep, pltpu.roll(depth, 1, 0)))

    centre = (lat * height + row).astype(F32) + 0.5
    coriolis = coriolis_coef * (2.0 * centre / (height * lat_n) - 1.0)
    spin = (0.25 * time_step) * coriolis
    tables = face_tables(levels)
    push = time_step * pressure_coef
    part = time_step * 0.5

    def density(t, s):
        return 0.8 * s - t * (1.0 + 0.1 * (t + s))

    def down(k, carry):
        heat, salt, zonal, merid, a, w, east_sum, north_sum = carry
        level = k.astype(F32) + 0.5
        t, s, u, v = fields[0, k], fields[1, k], fields[2, k], fields[3, k]
        te, tw, tn, ts = to_east_of(t, 0, k), to_west_of(t, 0, k), to_north_of(t, 0, k), to_south_of(t, 0, k)
        se, sw, sn, ss = to_east_of(s, 1, k), to_west_of(s, 1, k), to_north_of(s, 1, k), to_south_of(s, 1, k)
        ue, uw, un, us = to_east_of(u, 2, k), to_west_of(u, 2, k), to_north_of(u, 2, k), to_south_of(u, 2, k)
        ve, vw, vn, vs = to_east_of(v, 3, k), to_west_of(v, 3, k), to_north_of(v, 3, k), to_south_of(v, 3, k)
        uu, vv = u + uw, v + ve
        ubar = uu + to_north_of(uu, 4, k)
        vbar = vv + to_south_of(vv, 4, k)
        open_c = level < depth
        open_e, open_w = level < east_depth, level < west_depth
        open_n, open_s = level < north_depth, level < south_depth

        def face(mask, speed):
            x = part * speed
            return jnp.where(mask, part - x, 0.0), jnp.where(mask, part + x, 0.0)

        e_far, e_own = face(open_e, u)
        w_own, w_far = face(open_w, uw)
        n_far, n_own = face(open_n, v)
        s_own, s_far = face(open_s, vs)
        own = 1.0 - e_own - w_own - n_own - s_own
        t_star = own * t + e_far * te + w_far * tw + n_far * tn + s_far * ts
        s_star = own * s + e_far * se + w_far * sw + n_far * sn + s_far * ss

        rho = density(t, s)
        east_step = density(te, se) - rho
        north_step = density(tn, sn) - rho
        half_e = push * 0.5 * east_step
        half_n = push * 0.5 * north_step
        east_push = east_sum + half_e
        north_push = north_sum + half_n
        u_star = (1.0 - 4.0 * part) * u + part * (ue + uw + un + us) + spin * vbar - east_push
        v_star = (1.0 - 4.0 * part) * v + part * (ve + vw + vn + vs) - spin * ubar - north_push

        below = jnp.minimum(k, levels - 2)
        a_next = jnp.where(level + 1.0 < depth, time_step * mix[below], 0.0)
        d = (1.0 + a_next + a) - a * w
        r = pl.reciprocal(d, approx=True)
        r = r * (2.0 - d * r)
        w_next = a_next * r
        heat = jnp.where(open_c, (t_star + a * heat) * r, 0.0)
        salt = jnp.where(open_c, (s_star + a * salt) * r, 0.0)
        r_ahead, r_last = at_level(tables[0], k), at_level(tables[1], k)
        r_e = jnp.where(level + 1.0 < east_depth, r_ahead, r_last)
        r_n = jnp.where(level + 1.0 < north_depth, r_ahead, r_last)
        zonal = jnp.where(open_e, (u_star + part * zonal) * r_e, 0.0)
        merid = jnp.where(open_n, (v_star + part * merid) * r_n, 0.0)
        to_ref[k] = heat
        so_ref[k] = salt
        uo_ref[k] = zonal
        vo_ref[k] = merid
        w_ref[k] = w_next
        return heat, salt, zonal, merid, a_next, w_next, east_push + half_e, north_push + half_n

    state = (zero,) * 8
    for c in range(3):
        take_rows(c)
        state = lax.fori_loop(parts[c][0], parts[c][2], down, state, unroll=3)

    @pl.when(top)
    def _():
        for copy in to_mirror:
            copy.wait_send()

    @pl.when(inner)
    def _():
        for copy in to_north:
            copy.wait_send()

    @pl.when(has_south)
    def _():
        for copy in to_south:
            copy.wait_send()


def backward_kernel(to_ref, so_ref, uo_ref, vo_ref, w_ref, t_hbm, s_hbm, u_hbm, v_hbm, out, sem):
    levels, height, width = to_ref.shape
    factors = face_tables(levels)[2][1:]
    results = (t_hbm, s_hbm, u_hbm, v_hbm)
    heat, salt, zonal, merid = (ref[levels - 1] for ref in (to_ref, so_ref, uo_ref, vo_ref))
    for f, x in enumerate((heat, salt, zonal, merid)):
        out[f, levels - 1] = x

    def up(i, carry):
        heat, salt, zonal, merid = carry
        k = levels - 1 - i
        w = w_ref[k]
        wc = at_level(factors, k)
        heat = to_ref[k] + w * heat
        salt = so_ref[k] + w * salt
        zonal = uo_ref[k] + wc * zonal
        merid = vo_ref[k] + wc * merid
        for f, x in enumerate((heat, salt, zonal, merid)):
            out[f, k] = x
        return heat, salt, zonal, merid

    state = (heat, salt, zonal, merid)
    pieces = 4
    bounds = [levels * i // pieces for i in range(pieces + 1)]
    copies = []
    for i in range(pieces):
        state = lax.fori_loop(max(bounds[i], 1), bounds[i + 1], up, state, unroll=3)
        low, high = levels - bounds[i + 1], levels - bounds[i]
        for f in range(4):
            copy = pltpu.make_async_copy(out.at[f, low:high], results[f].at[low:high], sem.at[i, f])
            copy.start()
            copies.append(copy)
    for copy in copies:
        copy.wait()


def local(lon_n, lat_n, t, s, u, v, mix, h):
    levels, height, width = t.shape
    padded = (levels + 7) // 8 * 8
    vmem = pl.BlockSpec(memory_space=pltpu.VMEM)
    hbm = pl.BlockSpec(memory_space=pltpu.HBM)
    field = jax.ShapeDtypeStruct((levels, height, width), F32)
    dma = pltpu.SemaphoreType.DMA
    swept = pl.pallas_call(
        functools.partial(forward_kernel, lon_n, lat_n),
        out_shape=(field,) * 5,
        in_specs=[hbm] * 6,
        out_specs=(vmem,) * 5,
        scratch_shapes=[
            pltpu.VMEM((4, levels, height, width), F32),
            pltpu.VMEM((levels - 1, height, width), F32),
            pltpu.VMEM((height, width), jnp.int32),
            pltpu.VMEM((height, width), F32),
            pltpu.VMEM((2, height, width), F32),
            pltpu.VMEM((2, 4, padded, width), F32),
            pltpu.VMEM((2, 4, padded, width), F32),
            pltpu.VMEM((2, 4, height, width), F32),
            pltpu.VMEM((2, 4, height, width), F32),
            pltpu.VMEM((2, height, width), F32),
            pltpu.VMEM((5, padded, width), F32),
            pltpu.VMEM((5, padded, width), F32),
            dma((6,)), dma((2,)), dma((2,)), dma((2, 3)), dma((2, 3)),
            dma((2,)), dma((2,)), dma((2,)), dma((2,)), dma,
        ],
        compiler_params=pltpu.CompilerParams(
            collective_id=0, has_side_effects=True, vmem_limit_bytes=24 << 20),
    )(t, s, u, v, mix, h)
    return pl.pallas_call(
        backward_kernel,
        out_shape=(field,) * 4,
        in_specs=[vmem] * 5,
        out_specs=(hbm,) * 4,
        scratch_shapes=[pltpu.VMEM((4, levels, height, width), F32), dma((4, 4))],
        compiler_params=pltpu.CompilerParams(vmem_limit_bytes=16 << 20),
    )(*swept)


def solution(mesh):
    field = P(None, "lat", "lon")
    return jax.shard_map(
        functools.partial(local, mesh.shape["lon"], mesh.shape["lat"]),
        mesh=mesh,
        in_specs=(field,) * 5 + (P("lat", "lon"),),
        out_specs=(field,) * 4,
        check_vma=False,
    )
```

time: 21.8 us -> 22.7 us (1.041)
  Pallas kernels: 15.3 us -> 16.2 us
    pallas_call x2, Pallas kernels: 15.3 us -> 16.2 us  [the longest x1 14.9 us: local(): pl.pallas_call(functools.partial(forward_kernel, lon_n, lat_n), out_shape...]
    unnamed x20 -> x12, local copies, waits for them, and re-layouts: 5.52 us -> 5.5 us
where the time goes in v2:
time: 22.7 us; the launch traced here: 22.4 us
  Pallas kernels  16.2 us (71%)
  local copies, waits for them, and re-layouts  5.5 us (24%)
  between operations  0.65 us (3%)
    pallas_call x1, Pallas kernels, local(): pl.pallas_call(functools.partial(forward_kernel, lon_n, lat_n), out_shape...  14.9 us
    unnamed x12, local copies, waits for them, and re-layouts  5.5 us
    pallas_call x1, Pallas kernels, local(): pl.pallas_call(backward_kernel, out_shape=(field,) * 4, in_specs=[vmem] *...  1.3 us

profile of v2, /device:TPU:1, one launch (start us, length us, event | category | flops | bytes accessed | tf_op | source)
XLA Modules:
  0.0 22.4 jit_solution(8096532968976440774)
XLA Ops:
  0.6 0.0 copy-start
  0.6 1.0 %copy-done = f32[75,8,128]{2,1,0:T(8,128)S(1)} copy-done((f32[75,8,128]{2,1,0:T(8,128)S(1)}, f32[75,8,128]{2,1,0:T(8,128)}, u32[]{:S(2)}) %copy-start) | copy-done | bytes 307224
  1.6 0.0 copy-start.1
  1.6 1.0 %copy-done.1 = f32[75,8,128]{2,1,0:T(8,128)S(1)} copy-done((f32[75,8,128]{2,1,0:T(8,128)S(1)}, f32[75,8,128]{2,1,0:T(8,128)}, u32[]{:S(2)}) %copy-start.1) | copy-done | bytes 307224
  2.6 0.0 copy-start.2
  2.6 1.0 %copy-done.2 = f32[75,8,128]{2,1,0:T(8,128)S(1)} copy-done((f32[75,8,128]{2,1,0:T(8,128)S(1)}, f32[75,8,128]{2,1,0:T(8,128)}, u32[]{:S(2)}) %copy-start.2) | copy-done | bytes 307224
  3.5 0.0 copy-start.3
  3.5 1.0 %copy-done.3 = f32[75,8,128]{2,1,0:T(8,128)S(1)} copy-done((f32[75,8,128]{2,1,0:T(8,128)S(1)}, f32[75,8,128]{2,1,0:T(8,128)}, u32[]{:S(2)}) %copy-start.3) | copy-done | bytes 307224
  4.5 0.0 copy-start.4
  4.5 1.0 %copy-done.4 = f32[74,8,128]{2,1,0:T(8,128)S(1)} copy-done((f32[74,8,128]{2,1,0:T(8,128)S(1)}, f32[74,8,128]{2,1,0:T(8,128)}, u32[]{:S(2)}) %copy-start.4) | copy-done | bytes 303128
  5.5 0.0 copy-start.5
  5.5 0.7 %copy-done.5 = s32[8,128]{1,0:T(8,128)S(1)} copy-done((s32[8,128]{1,0:T(8,128)S(1)}, s32[8,128]{1,0:T(8,128)}, u32[]{:S(2)}) %copy-start.5) | copy-done | bytes 4120
  6.2 14.9 %shard_map.93 = (f32[75,8,128]{2,1,0:T(8,128)S(1)}, f32[75,8,128]{2,1,0:T(8,128)S(1)}, f32[75,8,128]{2,1,0:T(8,128)S(1)}, f32[75,8,128]{2,1,0:T(8,128)S(1)}, f32[75,8,128]{2,1,0:T(8,128)S(1)}) custom-call(f32[75,8,128]{2,1,0:T(8,128)S(1)} %copy-done, f32[75,8,128]{2,1,0:T(8,128)S(1)} %copy-done.1, f32[75,8,128]{2,1,0:T(8,128)S(1)} %copy-done.2, ...), custom_call_target="tpu_custom_call" | custom-call | tf_op jit(solution)/shard_map/pallas_call | solution.py:400
  21.1 1.3 %shard_map.94 = (f32[75,8,128]{2,1,0:T(8,128)}, f32[75,8,128]{2,1,0:T(8,128)}, f32[75,8,128]{2,1,0:T(8,128)}, f32[75,8,128]{2,1,0:T(8,128)}) custom-call(f32[75,8,128]{2,1,0:T(8,128)S(1)} %get-tuple-element.9.to_ref, f32[75,8,128]{2,1,0:T(8,128)S(1)} %get-tuple-element.10.so_ref, f32[75,8,128]{2,1,0:T(8,128)S(1)} %get-tuple-element.11.uo_ref, ...), custom_call_target="tpu_custom_call" | custom-call | tf_op jit(solution)/shard_map/pallas_call | solution.py:424
Async XLA Ops:
  0.6 1.0 %copy-start = (f32[75,8,128]{2,1,0:T(8,128)S(1)}, f32[75,8,128]{2,1,0:T(8,128)}, u32[]{:S(2)}) copy-start(f32[75,8,128]{2,1,0:T(8,128)} %t_hbm.1) | copy-start | bytes 921604
  1.6 1.0 %copy-start.1 = (f32[75,8,128]{2,1,0:T(8,128)S(1)}, f32[75,8,128]{2,1,0:T(8,128)}, u32[]{:S(2)}) copy-start(f32[75,8,128]{2,1,0:T(8,128)} %s_hbm.1) | copy-start | bytes 921604
  2.6 1.0 %copy-start.2 = (f32[75,8,128]{2,1,0:T(8,128)S(1)}, f32[75,8,128]{2,1,0:T(8,128)}, u32[]{:S(2)}) copy-start(f32[75,8,128]{2,1,0:T(8,128)} %u_hbm.1) | copy-start | bytes 921604
  3.5 1.0 %copy-start.3 = (f32[75,8,128]{2,1,0:T(8,128)S(1)}, f32[75,8,128]{2,1,0:T(8,128)}, u32[]{:S(2)}) copy-start(f32[75,8,128]{2,1,0:T(8,128)} %v_hbm.1) | copy-start | bytes 921604
  4.5 1.0 %copy-start.4 = (f32[74,8,128]{2,1,0:T(8,128)S(1)}, f32[74,8,128]{2,1,0:T(8,128)}, u32[]{:S(2)}) copy-start(f32[74,8,128]{2,1,0:T(8,128)} %mix_hbm.1) | copy-start | bytes 909316
  5.5 0.7 %copy-start.5 = (s32[8,128]{1,0:T(8,128)S(1)}, s32[8,128]{1,0:T(8,128)}, u32[]{:S(2)}) copy-start(s32[8,128]{1,0:T(8,128)} %h_hbm.1) | copy-start | bytes 12292

commit v3 on v2

--- a/solution.py
+++ b/solution.py
@@ -37,10 +37,7 @@
 
 
 def chunks(levels, padded):
-    size = padded // 3 // 8 * 8
-    starts = [i * size for i in range(3)]
-    stops = starts[1:] + [padded]
-    return [(a, b, min(b, levels)) for a, b in zip(starts, stops)]
+    return [(0, padded, levels)]
 
 
 def forward_kernel(lon_n, lat_n, t_hbm, s_hbm, u_hbm, v_hbm, mix_hbm, h_hbm,
@@ -100,12 +97,11 @@
             device_id={"lon": lon_to, "lat": lat_to}, device_id_type=MESH)
 
     def row_copy(c, own, slot, lon_to, lat_to):
-        a, b, _ = parts[c]
-        return remote(row_send.at[own, :, a:b], rows.at[slot, :, a:b], row_ss.at[own, c], row_rs.at[slot, c], lon_to, lat_to)
-
-    to_north = [row_copy(c, 1, 1, lon, lat + 1) for c in range(3)]
-    to_mirror = [row_copy(c, 1, 0, mirror, lat) for c in range(3)]
-    to_south = [row_copy(c, 0, 0, lon, lat - 1) for c in range(3)]
+        return remote(row_send.at[own, c], rows.at[slot, c], row_ss.at[own, c], row_rs.at[slot, c], lon_to, lat_to)
+
+    to_north = [row_copy(c, 1, 1, lon, lat + 1) for c in range(4)]
+    to_mirror = [row_copy(c, 1, 0, mirror, lat) for c in range(4)]
+    to_south = [row_copy(c, 0, 0, lon, lat - 1) for c in range(4)]
     to_north.append(remote(deep_send, deep_got.at[1], deep_ss.at[1], deep_rs.at[1], lon, lat + 1))
     to_mirror.append(remote(deep_send, deep_got.at[0], deep_ss.at[1], deep_rs.at[0], mirror, lat))
     to_south.append(remote(deep_send, deep_got.at[0], deep_ss.at[0], deep_rs.at[0], lon, lat - 1))
@@ -134,27 +130,28 @@
     loads[0].wait()
     depth = deep[...].astype(F32)
     deep_send[...] = depth
+    peers = (2 + 2 * has_south.astype(jnp.int32) + 2 * inner.astype(jnp.int32)
+             + top.astype(jnp.int32) + far.astype(jnp.int32))
+    pl.semaphore_wait(barrier, peers)
+    send_rows([4])
     for f in range(4):
         loads[1 + f].wait()
         row_send[0, f, :levels, :] = fields[f, :, 0, :]
         row_send[1, f, :levels, :] = fields[f, :, height - 1, :]
-
-    peers = (2 + 2 * has_south.astype(jnp.int32) + 2 * inner.astype(jnp.int32)
-             + top.astype(jnp.int32) + far.astype(jnp.int32))
-    pl.semaphore_wait(barrier, peers)
-    send_rows([3, 0])
+        send_rows([f])
+
 
     lane = lax.broadcasted_iota(jnp.int32, (height, width), 1)
     row = lax.broadcasted_iota(jnp.int32, (height, width), 0)
     zero = jnp.zeros((height, width), F32)
 
     def pack(k, packs):
-        here = lane == k
+        here, after = lane == k, lane == k + 1
         out = []
         for f in range(4):
-            x = fields[f, k]
-            out.append(jnp.where(here, pltpu.roll(x, k + 1, 1), packs[2 * f]))
-            out.append(jnp.where(here, pltpu.roll(x, k, 1), packs[2 * f + 1]))
+            moved = pltpu.roll(fields[f, k], k + 1, 1)
+            out.append(jnp.where(here, moved, packs[2 * f]))
+            out.append(jnp.where(after, moved, packs[2 * f + 1]))
         return tuple(out)
 
     packs = lax.fori_loop(0, levels, pack, (zero,) * 8, unroll=5)
@@ -162,7 +159,7 @@
         for side in range(2):
             tile = packs[2 * f + side]
             if f == 0:
-                tile = jnp.where(lane == levels, pltpu.roll(depth, levels + 1 - side, 1), tile)
+                tile = jnp.where(lane == levels + side, pltpu.roll(depth, levels + 1, 1), tile)
             col_send[side, f] = tile
 
     to_east.start()
@@ -184,7 +181,6 @@
     def _():
         to_south_east.start()
 
-    send_rows([1, 2])
 
     first_lane, last_lane = lane == 0, lane == width - 1
     first_row, last_row = row == 0, row == height - 1
@@ -210,26 +206,28 @@
     def _():
         to_north_west.wait_recv()
         to_south_east.wait_send()
-        to_north[3].wait_recv()
+        to_north[4].wait_recv()
 
     @pl.when(far)
     def _():
         to_second.wait()
 
-    to_south[3].wait_recv()
+    to_south[4].wait_recv()
     north_deep = turned(jnp.where(top, pltpu.roll(deep_got[0], 1, 0), deep_got[0]))[:1]
     south_deep = jnp.where(has_south, deep_got[1], 0.0)[height - 1 :]
     north_corner = jnp.where(top, corners[0, height - 1 :, :], corners[0, :1, :])
     north_corner = jnp.transpose(jnp.broadcast_to(north_corner, (width, width)))[:padded]
-    south_corner = jnp.transpose(jnp.broadcast_to(corners[1, height - 1 :, :], (width, width)))[:padded]
+    south_corner = jnp.transpose(jnp.broadcast_to(pltpu.roll(corners[1], width - 1, 1)[height - 1 :], (width, width)))[:padded]
 
     def take_rows(c):
         a, b, _ = parts[c]
-        to_south[c].wait_recv()
+        for i in range(4):
+            to_south[i].wait_recv()
 
         @pl.when(has_south)
         def _():
-            to_north[c].wait_recv()
+            for i in range(4):
+                to_north[i].wait_recv()
 
         wide_lane = lax.broadcasted_iota(jnp.int32, (b - a, width), 1)
         corner = north_corner[a:b]
@@ -250,7 +248,7 @@
         south_ref[4, a:b] = jnp.where(has_south, merid + ahead, 0.0)
 
     def to_east_of(x, f, k):
-        return jnp.where(last_lane, pltpu.roll(cols[1, f], width - 1 - k, 1), pltpu.roll(x, width - 1, 1))
+        return jnp.where(last_lane, pltpu.roll(cols[1, f], width - 2 - k, 1), pltpu.roll(x, width - 1, 1))
 
     def to_west_of(x, f, k):
         return jnp.where(first_lane, pltpu.roll(cols[0, f], lax.rem(width - k, width), 1), pltpu.roll(x, 1, 1))
@@ -334,7 +332,7 @@
         return heat, salt, zonal, merid, a_next, w_next, east_push + half_e, north_push + half_n
 
     state = (zero,) * 8
-    for c in range(3):
+    for c in range(len(parts)):
         take_rows(c)
         state = lax.fori_loop(parts[c][0], parts[c][2], down, state, unroll=3)
 
@@ -397,6 +395,7 @@
     hbm = pl.BlockSpec(memory_space=pltpu.HBM)
     field = jax.ShapeDtypeStruct((levels, height, width), F32)
     dma = pltpu.SemaphoreType.DMA
+    t, s, u, v, mix, h = (pltpu.with_memory_space_constraint(x, pltpu.HBM) for x in (t, s, u, v, mix, h))
     swept = pl.pallas_call(
         functools.partial(forward_kernel, lon_n, lat_n),
         out_shape=(field,) * 5,
@@ -415,7 +414,7 @@
             pltpu.VMEM((2, height, width), F32),
             pltpu.VMEM((5, padded, width), F32),
             pltpu.VMEM((5, padded, width), F32),
-            dma((6,)), dma((2,)), dma((2,)), dma((2, 3)), dma((2, 3)),
+            dma((6,)), dma((2,)), dma((2,)), dma((2, 4)), dma((2, 4)),
             dma((2,)), dma((2,)), dma((2,)), dma((2,)), dma,
         ],
         compiler_params=pltpu.CompilerParams(

time: 22.7 us -> 16.7 us (0.74)
  local copies, waits for them, and re-layouts: 5.5 us -> 0 us
  Pallas kernels: 16.2 us -> 15.9 us
    unnamed x12 -> x0, local copies, waits for them, and re-layouts: 5.5 us -> none
    pallas_call x1, Pallas kernels: 14.9 us -> 14.6 us  [local(): pl.pallas_call(functools.partial(forward_kernel, lon_n, lat_n), out_shape...]
where the time goes in v3:
time: 16.7 us; the launch traced here: 16.5 us
  Pallas kernels  15.9 us (95%)
  between operations  0.64 us (4%)
    pallas_call x1, Pallas kernels, local(): pl.pallas_call(functools.partial(forward_kernel, lon_n, lat_n), out_shape...  14.6 us
    pallas_call x1, Pallas kernels, local(): pl.pallas_call(backward_kernel, out_shape=(field,) * 4, in_specs=[vmem] *...  1.3 us

profile of v3, /device:TPU:1, one launch (start us, length us, event | category | flops | bytes accessed | tf_op | source)
XLA Modules:
  0.0 16.5 jit_solution(7803839854224445851)
XLA Ops:
  0.6 14.6 %shard_map.93 = (f32[75,8,128]{2,1,0:T(8,128)S(1)}, f32[75,8,128]{2,1,0:T(8,128)S(1)}, f32[75,8,128]{2,1,0:T(8,128)S(1)}, f32[75,8,128]{2,1,0:T(8,128)S(1)}, f32[75,8,128]{2,1,0:T(8,128)S(1)}) custom-call(f32[75,8,128]{2,1,0:T(8,128)} %t_hbm.1, f32[75,8,128]{2,1,0:T(8,128)} %s_hbm.1, f32[75,8,128]{2,1,0:T(8,128)} %u_hbm.1, f32[75,8,128]{2,1,0:T(8,128)} %v_hbm.1, ...), custom_call_target="tpu_custom_call" | custom-call | tf_op jit(solution)/shard_map/pallas_call | solution.py:399
  15.2 1.3 %shard_map.94 = (f32[75,8,128]{2,1,0:T(8,128)}, f32[75,8,128]{2,1,0:T(8,128)}, f32[75,8,128]{2,1,0:T(8,128)}, f32[75,8,128]{2,1,0:T(8,128)}) custom-call(f32[75,8,128]{2,1,0:T(8,128)S(1)} %get-tuple-element.9.to_ref, f32[75,8,128]{2,1,0:T(8,128)S(1)} %get-tuple-element.10.so_ref, f32[75,8,128]{2,1,0:T(8,128)S(1)} %get-tuple-element.11.uo_ref, ...), custom_call_target="tpu_custom_call" | custom-call | tf_op jit(solution)/shard_map/pallas_call | solution.py:423

commit v4 on v3

--- a/solution.py
+++ b/solution.py
@@ -36,18 +36,13 @@
     return value
 
 
-def chunks(levels, padded):
-    return [(0, padded, levels)]
-
-
 def forward_kernel(lon_n, lat_n, t_hbm, s_hbm, u_hbm, v_hbm, mix_hbm, h_hbm,
                    to_ref, so_ref, uo_ref, vo_ref, w_ref,
                    fields, mix, deep, deep_send, deep_got, row_send, rows, col_send, cols, corners,
-                   north_ref, south_ref,
+                   north_ref, south_ref, above_ref, r_ref,
                    in_sem, deep_ss, deep_rs, row_ss, row_rs, col_ss, col_rs, cor_ss, cor_rs, fold_ss):
     levels, height, width = t_hbm.shape
     padded = rows.shape[2]
-    parts = chunks(levels, padded)
     lon = lax.axis_index("lon")
     lat = lax.axis_index("lat")
     east = lax.rem(lon + 1, lon_n)
@@ -199,7 +194,6 @@
 
     @pl.when(inner)
     def _():
-        to_south_east.wait_recv()
         to_north_west.wait_send()
 
     @pl.when(has_south)
@@ -208,27 +202,40 @@
         to_south_east.wait_send()
         to_north[4].wait_recv()
 
-    @pl.when(far)
-    def _():
-        to_second.wait()
-
     to_south[4].wait_recv()
     north_deep = turned(jnp.where(top, pltpu.roll(deep_got[0], 1, 0), deep_got[0]))[:1]
     south_deep = jnp.where(has_south, deep_got[1], 0.0)[height - 1 :]
-    north_corner = jnp.where(top, corners[0, height - 1 :, :], corners[0, :1, :])
-    north_corner = jnp.transpose(jnp.broadcast_to(north_corner, (width, width)))[:padded]
     south_corner = jnp.transpose(jnp.broadcast_to(pltpu.roll(corners[1], width - 1, 1)[height - 1 :], (width, width)))[:padded]
 
-    def take_rows(c):
-        a, b, _ = parts[c]
+    a, b = 0, padded
+
+    def take_south():
+        @pl.when(has_south)
+        def _():
+            for i in range(4):
+                to_north[i].wait_recv()
+
+        wide_lane = lax.broadcasted_iota(jnp.int32, (b - a, width), 1)
+        merid = rows[1, 3, a:b]
+        for f in range(4):
+            south_ref[f, a:b] = jnp.where(has_south, rows[1, f, a:b], 0.0)
+        ahead = jnp.where(wide_lane == width - 1, south_corner[a:b], pltpu.roll(merid, width - 1, 1))
+        south_ref[4, a:b] = jnp.where(has_south, merid + ahead, 0.0)
+
+    def take_north():
         for i in range(4):
             to_south[i].wait_recv()
 
-        @pl.when(has_south)
-        def _():
-            for i in range(4):
-                to_north[i].wait_recv()
-
+        @pl.when(inner)
+        def _():
+            to_south_east.wait_recv()
+
+        @pl.when(far)
+        def _():
+            to_second.wait()
+
+        north_corner = jnp.where(top, corners[0, height - 1 :, :], corners[0, :1, :])
+        north_corner = jnp.transpose(jnp.broadcast_to(north_corner, (width, width)))[:padded]
         wide_lane = lax.broadcasted_iota(jnp.int32, (b - a, width), 1)
         corner = north_corner[a:b]
         north_ref[0, a:b] = turned(rows[0, 0, a:b])
@@ -241,11 +248,6 @@
         north_ref[2, a:b] = sign * here
         north_ref[3, a:b] = sign * turned(rows[0, 3, a:b])
         north_ref[4, a:b] = sign * (here + behind)
-        merid = rows[1, 3, a:b]
-        for f in range(4):
-            south_ref[f, a:b] = jnp.where(has_south, rows[1, f, a:b], 0.0)
-        ahead = jnp.where(wide_lane == width - 1, south_corner[a:b], pltpu.roll(merid, width - 1, 1))
-        south_ref[4, a:b] = jnp.where(has_south, merid + ahead, 0.0)
 
     def to_east_of(x, f, k):
         return jnp.where(last_lane, pltpu.roll(cols[1, f], width - 2 - k, 1), pltpu.roll(x, width - 1, 1))
@@ -254,7 +256,7 @@
         return jnp.where(first_lane, pltpu.roll(cols[0, f], lax.rem(width - k, width), 1), pltpu.roll(x, 1, 1))
 
     def to_north_of(x, f, k):
-        return jnp.where(last_row, north_ref[f, pl.ds(k, 1), :], pltpu.roll(x, height - 1, 0))
+        return jnp.where(last_row, 0.0, pltpu.roll(x, height - 1, 0))
 
     def to_south_of(x, f, k):
         return jnp.where(first_row, south_ref[f, pl.ds(k, 1), :], pltpu.roll(x, 1, 0))
@@ -275,7 +277,7 @@
         return 0.8 * s - t * (1.0 + 0.1 * (t + s))
 
     def down(k, carry):
-        heat, salt, zonal, merid, a, w, east_sum, north_sum = carry
+        a, w, east_sum, north_sum = carry
         level = k.astype(F32) + 0.5
         t, s, u, v = fields[0, k], fields[1, k], fields[2, k], fields[3, k]
         te, tw, tn, ts = to_east_of(t, 0, k), to_west_of(t, 0, k), to_north_of(t, 0, k), to_south_of(t, 0, k)
@@ -317,24 +319,43 @@
         r = pl.reciprocal(d, approx=True)
         r = r * (2.0 - d * r)
         w_next = a_next * r
-        heat = jnp.where(open_c, (t_star + a * heat) * r, 0.0)
-        salt = jnp.where(open_c, (s_star + a * salt) * r, 0.0)
+        to_ref[k] = t_star
+        so_ref[k] = s_star
+        uo_ref[k] = u_star
+        vo_ref[k] = v_star
+        w_ref[k] = w_next
+        above_ref[k] = a
+        r_ref[k] = jnp.where(open_c, r, 0.0)
+        return a_next, w_next, east_push + half_e, north_push + half_n
+
+    def solve(k, carry):
+        heat, salt, zonal, merid, north_sum = carry
+        level = k.astype(F32) + 0.5
+        open_e, open_n = level < east_depth, level < north_depth
+        tn, sn, un, vn, uq = (jnp.where(last_row, north_ref[f, pl.ds(k, 1), :], 0.0) for f in range(5))
+        n_far = jnp.where(open_n, part - part * fields[3, k], 0.0)
+        half = push * 0.5 * density(tn, sn)
+        north_push = north_sum + half
+        a, r = above_ref[k], r_ref[k]
+        u_star = uo_ref[k] + part * un
+        v_star = vo_ref[k] + part * vn - spin * uq - north_push
         r_ahead, r_last = at_level(tables[0], k), at_level(tables[1], k)
         r_e = jnp.where(level + 1.0 < east_depth, r_ahead, r_last)
         r_n = jnp.where(level + 1.0 < north_depth, r_ahead, r_last)
+        heat = (to_ref[k] + n_far * tn + a * heat) * r
+        salt = (so_ref[k] + n_far * sn + a * salt) * r
         zonal = jnp.where(open_e, (u_star + part * zonal) * r_e, 0.0)
         merid = jnp.where(open_n, (v_star + part * merid) * r_n, 0.0)
         to_ref[k] = heat
         so_ref[k] = salt
         uo_ref[k] = zonal
         vo_ref[k] = merid
-        w_ref[k] = w_next
-        return heat, salt, zonal, merid, a_next, w_next, east_push + half_e, north_push + half_n
-
-    state = (zero,) * 8
-    for c in range(len(parts)):
-        take_rows(c)
-        state = lax.fori_loop(parts[c][0], parts[c][2], down, state, unroll=3)
+        return heat, salt, zonal, merid, north_push + half
+
+    take_south()
+    lax.fori_loop(0, levels, down, (zero,) * 4, unroll=3)
+    take_north()
+    lax.fori_loop(0, levels, solve, (zero,) * 5, unroll=3)
 
     @pl.when(top)
     def _():
@@ -414,6 +435,8 @@
             pltpu.VMEM((2, height, width), F32),
             pltpu.VMEM((5, padded, width), F32),
             pltpu.VMEM((5, padded, width), F32),
+            pltpu.VMEM((levels, height, width), F32),
+            pltpu.VMEM((levels, height, width), F32),
             dma((6,)), dma((2,)), dma((2,)), dma((2, 4)), dma((2, 4)),
             dma((2,)), dma((2,)), dma((2,)), dma((2,)), dma,
         ],

time: 16.7 us -> 17.2 us (1.030)
  the two profiles are of different devices: /device:TPU:1 before, /device:TPU:0 now
where the time goes in v4:
time: 17.2 us; the launch traced here: 17 us
  Pallas kernels  16.4 us (95%)
  between operations  0.64 us (4%)
    pallas_call x1, Pallas kernels, local(): pl.pallas_call(functools.partial(forward_kernel, lon_n, lat_n), out_shape...  15.1 us
    pallas_call x1, Pallas kernels, local(): pl.pallas_call(backward_kernel, out_shape=(field,) * 4, in_specs=[vmem] *...  1.3 us

profile of v4, /device:TPU:0, one launch (start us, length us, event | category | flops | bytes accessed | tf_op | source)
XLA Modules:
  0.0 17.0 jit_solution(235974432562408416)
XLA Ops:
  0.6 15.1 %shard_map.93 = (f32[75,8,128]{2,1,0:T(8,128)S(1)}, f32[75,8,128]{2,1,0:T(8,128)S(1)}, f32[75,8,128]{2,1,0:T(8,128)S(1)}, f32[75,8,128]{2,1,0:T(8,128)S(1)}, f32[75,8,128]{2,1,0:T(8,128)S(1)}) custom-call(f32[75,8,128]{2,1,0:T(8,128)} %t_hbm.1, f32[75,8,128]{2,1,0:T(8,128)} %s_hbm.1, f32[75,8,128]{2,1,0:T(8,128)} %u_hbm.1, f32[75,8,128]{2,1,0:T(8,128)} %v_hbm.1, ...), custom_call_target="tpu_custom_call" | custom-call | tf_op jit(solution)/shard_map/pallas_call | solution.py:420
  15.7 1.3 %shard_map.94 = (f32[75,8,128]{2,1,0:T(8,128)}, f32[75,8,128]{2,1,0:T(8,128)}, f32[75,8,128]{2,1,0:T(8,128)}, f32[75,8,128]{2,1,0:T(8,128)}) custom-call(f32[75,8,128]{2,1,0:T(8,128)S(1)} %get-tuple-element.9.to_ref, f32[75,8,128]{2,1,0:T(8,128)S(1)} %get-tuple-element.10.so_ref, f32[75,8,128]{2,1,0:T(8,128)S(1)} %get-tuple-element.11.uo_ref, ...), custom_call_target="tpu_custom_call" | custom-call | tf_op jit(solution)/shard_map/pallas_call | solution.py:446
